TPU v7x, 256 devices: a whole 4x4x8 slice. The times are simulated.
256 devices in a mesh: scan: 64 (over x, y, z_lo, core), tile: 4 (over z_hi).
Axes of the slice: x: 4, y: 4, z: 8 (z_hi: 4, z_lo: 2; z = z_hi * 2 + z_lo), core: 2. Of those that a mesh axis runs over, the one named last changes fastest.
Arguments:
- object_field: float32 [2, 16384, 1024], P(None, 'scan', 'tile'), may hold values from -4.2 to 4.2
- probe_modes: float32 [8, 2, 256, 256], P('tile'), may hold values from -2.1 to 2.1
- amplitudes: bfloat16 [512, 256, 256], P('scan'), may hold values from 0.25 to 3
- positions: int32 [512, 2], P('scan'), may hold values from 0 to 16128, as said below
- counts: int32 [64], P('scan'), may hold values from 1 to 8, as said below
Outputs:
- new_object: float32 [2, 16384, 1024], P(None, 'scan', 'tile')
- probe_step: float32 [8, 2, 256, 256], P('tile')
Inputs may be any that keep to these rules, and one draw needn't show every extreme that they name: `positions`: slot j's row offset lies in rows (j // 8) * 256 to (j // 8) * 256 + 255; every window lies inside the object: row offsets at most 16128, column offsets at most 768. `counts`: some scan index holds 8 live slots and some holds one.
All inputs are finite; a program needn't handle non-finite values.
Results may differ from a plain program's by a relative error of at most 0.003.
Values may be sent and summed in bfloat16 or wider, within the bound.
A program may use at most 128 MiB of HBM per device.

v0:
```python
import math

import jax
import jax.numpy as jnp
from jax import lax
from jax.sharding import PartitionSpec as P

damping = 1.0
amp_floor = 0.5


def passed_along(value, axis, steps):
    count = lax.axis_size(axis)
    leading, last = (max(0, -steps), min(count, count - steps))
    return lax.ppermute(value, axis, [(source, source + steps) for source in range(leading, last)])


def dft_tables(win_width):
    index_row = jnp.arange(win_width, dtype=jnp.int32)
    products = index_row[:, None] * index_row[None, :] % win_width
    phase_angle = products.astype(jnp.float32) * (2.0 * math.pi / win_width)
    norm_scale = 1.0 / math.sqrt(win_width)
    real_part = (jnp.cos(phase_angle) * norm_scale).astype(jnp.bfloat16)
    imag_part = (-jnp.sin(phase_angle) * norm_scale).astype(jnp.bfloat16)
    return (real_part, imag_part)


def transform(rowform, right_table, left_table, win_width):
    half_done = jnp.einsum(
        "mak,kl->mal", rowform, right_table, preferred_element_type=jnp.float32
    ).astype(jnp.bfloat16)
    full_block = jnp.einsum(
        "ca,mak->mck", left_table, half_done, preferred_element_type=jnp.float32
    )
    real_out = full_block[..., :win_width, :win_width] - full_block[..., win_width:, win_width:]
    imag_out = full_block[..., :win_width, win_width:] + full_block[..., win_width:, :win_width]
    return (real_out, imag_out)


def shards(object_field, probe_modes, amplitudes, positions, counts):
    slot_count = amplitudes.shape[0]
    win_width = amplitudes.shape[1]
    band_rows = object_field.shape[1]
    first_row = lax.axis_index("scan") * band_rows
    object_low = object_field.astype(jnp.bfloat16)
    lower_rows = passed_along(object_low, "scan", -1)
    extended = jnp.concatenate([object_low, lower_rows], axis=1)
    band_all = lax.all_gather(extended, "tile", axis=2, tiled=True)
    row_offsets = positions[:, 0] - first_row
    col_offsets = positions[:, 1]
    zero_index = jnp.zeros((), jnp.int32)

    def cut_window(row_at, col_at):
        return lax.dynamic_slice(band_all, (zero_index, row_at, col_at), (2, win_width, win_width))

    windows = jax.vmap(cut_window)(row_offsets, col_offsets)
    slot_ids = jnp.arange(slot_count, dtype=jnp.int32)
    live_mask = (slot_ids < counts[0]).astype(jnp.float32)
    real_part, imag_part = dft_tables(win_width)
    right_fwd = jnp.block([[real_part, imag_part], [-imag_part, real_part]])
    left_fwd = jnp.concatenate([real_part, imag_part], axis=0)
    right_inv = jnp.block([[real_part, -imag_part], [imag_part, real_part]])
    left_inv = jnp.concatenate([real_part, -imag_part], axis=0)
    probe_re = probe_modes[:, 0]
    probe_im = probe_modes[:, 1]
    probe_power = jnp.sum(probe_re * probe_re + probe_im * probe_im, axis=0)

    def forward_one(window):
        window_re = window[0].astype(jnp.float32)
        window_im = window[1].astype(jnp.float32)
        exit_wave = jnp.concatenate(
            [
                probe_re * window_re - probe_im * window_im,
                probe_re * window_im + probe_im * window_re,
            ],
            axis=-1,
        ).astype(jnp.bfloat16)
        far_re, far_im = transform(exit_wave, right_fwd, left_fwd, win_width)
        return (far_re, far_im, jnp.sum(far_re * far_re + far_im * far_im, axis=0))

    far_re, far_im, local_power = lax.map(forward_one, windows)
    intensity = lax.psum(local_power, "tile")
    factor = live_mask[:, None, None] * (
        amplitudes.astype(jnp.float32) / jnp.maximum(jnp.sqrt(intensity), amp_floor) - 1.0
    )
    channels = 3

    def accumulate(running, inputs):
        buffer, grad_sum, weight_sum = running
        slot_re, slot_im, slot_factor, window, live, row_at, col_at = inputs
        change = jnp.concatenate([slot_factor * slot_re, slot_factor * slot_im], axis=-1).astype(
            jnp.bfloat16
        )
        near_re, near_im = transform(change, right_inv, left_inv, win_width)
        window_re = window[0].astype(jnp.float32)
        window_im = window[1].astype(jnp.float32)
        numer_parts = [
            jnp.sum(probe_re * near_re + probe_im * near_im, axis=0),
            jnp.sum(probe_re * near_im - probe_im * near_re, axis=0),
        ]
        numer_parts.append(live * probe_power)
        numer = jnp.stack(numer_parts)
        grads = jnp.stack(
            [window_re * near_re + window_im * near_im, window_re * near_im - window_im * near_re],
            axis=1,
        )
        weight = window_re * window_re + window_im * window_im
        region = lax.dynamic_slice(
            buffer, (zero_index, row_at, col_at), (channels, win_width, win_width)
        )
        buffer = lax.dynamic_update_slice(buffer, region + numer, (zero_index, row_at, col_at))
        return ((buffer, grad_sum + grads, weight_sum + live * weight), None)

    init = (
        jnp.zeros((channels, band_rows + win_width, band_all.shape[2]), jnp.float32),
        jnp.zeros(probe_modes.shape, jnp.float32),
        jnp.zeros((win_width, win_width), jnp.float32),
    )
    (buffer, grad_sum, weight_sum), _ = lax.scan(
        accumulate, init, (far_re, far_im, factor, windows, live_mask, row_offsets, col_offsets)
    )
    col_sums = lax.psum_scatter(buffer, "tile", scatter_dimension=2, tiled=True)
    rim_rows = passed_along(col_sums[:, band_rows:, :], "scan", 1)
    totals = col_sums[:, :band_rows, :].at[:, :win_width, :].add(rim_rows)
    illumination = totals[2]
    new_object = object_field + totals[0:2] / (illumination + damping)[None]
    grad_total, weight_total = lax.psum((grad_sum, weight_sum), "scan")
    probe_step = grad_total / (weight_total + damping)[None, None]
    return (new_object, probe_step)


def solution(mesh):
    placed = (
        P(None, "scan", "tile"),
        P("tile", None, None, None),
        P("scan", None, None),
        P("scan", None),
        P("scan"),
    )
    return jax.shard_map(
        shards,
        mesh=mesh,
        in_specs=placed,
        out_specs=(P(None, "scan", "tile"), P("tile", None, None, None)),
        check_vma=False,
    )
```

profile of v0, /device:TPU:1, one launch (start us, length us, event | category | flops | bytes accessed | tf_op | source)
XLA Modules:
  0.0 1201.8 jit_solution(13292454651381135807)
XLA Ops:
  8.3 5.3 collective-permute-start
  13.6 3.8 collective-permute-done
  23.5 54.8 %all-gather.2.cloned.1.call-done = bf16[2,512,1024]{2,1,0:T(8,128)(2,1)} async-done(((bf16[2,512,256]{2,1,0:T(8,128)(2,1)}), bf16[2,512,1024]{2,1,0:T(8,128)(2,1)}) %all-gather.2.cloned.1.call-update) | async-done | bytes 2097168 | tf_op jit(solution)/shard_map/all_gather | solution.py:48
  78.4 29.4 %while.33 = (s32[]{:T(128)}, bf16[2,512,1024]{2,1,0:T(8,128)(2,1)}, s32[8,3]{0,1:T(4,128)S(1)}, bf16[8,2,256,256]{3,2,1,0:T(8,128)(2,1)}, s32[]{:T(128)}) while((s32[]{:T(128)}, bf16[2,512,1024]{2,1,0:T(8,128)(2,1)}, s32[8,3]{0,1:T(4,128)S(1)}, bf16[8,2,256,256]{3,2,1,0:T(8,128)(2,1)}, s32[]{:T(128)}) %tuple.102), condition=%wide.while_cond.1, body=%wide.while_body.1.sunk | while | flops 2 | bytes 525429 | solution.py:54
  78.9 3.1 bitcast_dynamic-update-slice_fusion.6
  82.6 3.1 bitcast_dynamic-update-slice_fusion.6
  86.3 3.1 bitcast_dynamic-update-slice_fusion.6
  90.0 3.1 bitcast_dynamic-update-slice_fusion.6
  93.6 3.1 bitcast_dynamic-update-slice_fusion.6
  97.3 3.1 bitcast_dynamic-update-slice_fusion.6
  101.0 3.1 bitcast_dynamic-update-slice_fusion.6
  104.6 3.1 bitcast_dynamic-update-slice_fusion.6
  107.7 41.9 %while.32 = (s32[]{:T(128)}, f32[8,2,256,256]{2,3,1,0:T(8,128)}, f32[8,2,256,256]{2,3,1,0:T(8,128)}, f32[8,256,256]{2,1,0:T(8,128)}, bf16[8,2,256,256]{3,2,1,0:T...) while((s32[]{:T(128)}, f32[8,2,256,256]{2,3,1,0:T(8,128)}, ...), condition=%wide.region_2.3_spmd, body=%wide.region_0.2_spmd.sunk | while | flops 540344320 | bytes 12845209 | solution.py:81
  154.7 93.4 %all-reduce.4.cloned.1.call-done = f32[8,256,256]{2,1,0:T(8,128)} async-done(((f32[8,256,256]{2,1,0:T(8,128)}), f32[8,256,256]{2,1,0:T(8,128)}) %all-reduce.4.cloned.1.call-update) | async-done | bytes 2097168 | tf_op jit(solution)/shard_map/psum | solution.py:82
  248.1 3.8 add_multiply_fusion
  251.9 3.4 broadcast_in_dim.23.clone
  255.4 273.8 %while.34 = (s32[]{:T(128)}, f32[3,512,1024]{2,1,0:T(8,128)}, f32[2,2,256,256]{2,3,0,1:T(8,128)}, f32[256,256]{0,1:T(8,128)}, s32[8]{0:T(128)S(1)}, /*index=5*/s...) while((s32[]{:T(128)}, f32[3,512,1024]{2,1,0:T(8,128)}, ...), condition=%wide.region_8.9_spmd.clone, body=%wide.region_5.8_spmd.clone.sunk | while | flops 542769152 | bytes 35914140 | solution.py:119
  264.2 2.4 multiply_bitcast_fusion.2
  278.6 8.8 dynamic_update_slice.23
  294.8 2.4 select_add_fusion.2
  297.2 2.4 multiply_bitcast_fusion.2
  310.6 2.3 maximum_add_fusion.5
  312.9 9.3 dynamic_update_slice.23
  329.5 2.4 select_add_fusion.2
  331.9 2.4 multiply_bitcast_fusion.2
  345.3 2.3 maximum_add_fusion.5
  347.6 8.8 dynamic_update_slice.23
  363.8 2.4 select_add_fusion.2
  366.2 2.4 multiply_bitcast_fusion.2
  379.6 2.3 maximum_add_fusion.5
  381.9 8.8 dynamic_update_slice.23
  398.0 2.4 select_add_fusion.2
  400.4 2.4 multiply_bitcast_fusion.2
  413.8 2.3 maximum_add_fusion.5
  416.1 8.6 dynamic_update_slice.23
  432.1 2.4 select_add_fusion.2
  434.5 2.4 multiply_bitcast_fusion.2
  447.9 2.3 maximum_add_fusion.5
  450.2 9.3 dynamic_update_slice.23
  466.9 2.4 select_add_fusion.2
  469.3 2.4 multiply_bitcast_fusion.2
  485.0 9.4 dynamic_update_slice.23
  501.8 2.4 select_add_fusion.2
  504.2 2.4 multiply_bitcast_fusion.2
  519.9 9.3 dynamic_update_slice.23
  531.7 116.5 %reduce-scatter.2.cloned.1.call-done = f32[3,512,256]{2,1,0:T(8,128)} async-done(((f32[3,512,1024]{2,1,0:T(8,128)}), f32[3,512,256]{2,1,0:T(8,128)}) %reduce-scatter.2.cloned.1.call-update) | async-done | bytes 1572880 | tf_op jit(solution)/shard_map/reduce_scatter | solution.py:122
  651.5 538.2 %all-reduce.6.cloned.1.call-done = (f32[2,2,256,256]{3,2,1,0:T(8,128)}, f32[256,256]{0,1:T(8,128)}) async-done(((f32[2,2,256,256]{3,2,1,0:T(8,128)}, f32[256,256]{0,1:T(8,128)}), (f32[2,2,256,256]{3,2,1,0:T(8,128)}, f32[256,256]{0,1:T(8,128)})) %all-reduce.6.cloned.1.call-update) | async-done | bytes 1310736 | tf_op jit(solution)/shard_map/psum | solution.py:127
  1190.8 2.4 broadcast_divide_fusion
  (313 shorter events, 186.8 us)
Async XLA Ops:
  7.2 11.2 copy-start.9
  7.2 71.2 %all-gather.2.cloned.1.call-start = ((), (), s32[]{:S(2)}) async-start(), calls=%async_computation.1 | async-start | bytes 2621440 | tf_op jit(solution)/shard_map/all_gather | solution.py:48
  8.3 13.8 %copy-start.7 = (f32[2,2,256,256]{3,2,1,0:T(8,128)S(1)}, f32[2,2,256,256]{3,2,1,0:T(8,128)}, u32[]{:S(2)}) copy-start(f32[2,2,256,256]{3,2,1,0:T(8,128)} %param.14) | copy-start | bytes 3145732
  8.3 9.1 collective-permute-start
  18.3 229.8 %all-reduce.4.cloned.1.call-start = ((), (), s32[]{:S(2)}) async-start(), calls=%async_computation.2 | async-start | bytes 4194304 | tf_op jit(solution)/shard_map/psum | solution.py:82
  149.6 1.0 copy-start.5
  149.6 2.0 copy-start.4
  149.6 98.5 %copy-start.8 = (bf16[8,256,256]{2,1,0:T(8,128)(2,1)S(1)}, bf16[8,256,256]{2,1,0:T(8,128)(2,1)}, u32[]{:S(2)}) copy-start(bf16[8,256,256]{2,1,0:T(8,128)(2,1)} %param.15) | copy-start | bytes 3145732
  149.6 498.6 %reduce-scatter.2.cloned.1.call-start = ((), (), s32[]{:S(2)}) async-start(), calls=%async_computation.3 | async-start | bytes 7864320 | tf_op jit(solution)/shard_map/reduce_scatter | solution.py:122
  275.0 1.5 copy-start.2
  276.5 1.0 copy-start
  308.0 1.5 copy-start.2
  309.5 1.0 copy-start
  342.7 1.5 copy-start.2
  344.2 1.0 copy-start
  377.0 1.5 copy-start.2
  378.5 1.0 copy-start
  411.2 1.5 copy-start.2
  412.8 1.0 copy-start
  445.3 1.5 copy-start.2
  446.8 1.0 copy-start
  480.1 1.5 copy-start.2
  481.6 1.0 copy-start
  515.0 1.5 copy-start.2
  516.5 1.0 copy-start
  529.2 1.2 copy-start.1
  529.2 660.5 %all-reduce.6.cloned.1.call-start = ((), (), s32[]{:S(2)}) async-start(), calls=%async_computation.4 | async-start | bytes 2621440 | tf_op jit(solution)/shard_map/psum | solution.py:127
  649.4 543.7 %copy-start.6 = (f32[3,512,256]{2,1,0:T(8,128)S(1)}, f32[3,512,256]{2,1,0:T(8,128)}, u32[]{:S(2)}) copy-start(f32[3,512,256]{2,1,0:T(8,128)} %reduce-scatter.2.cloned.1.call-done) | copy-start | bytes 4718596
  649.4 543.7 %collective-permute-start.1 = (f32[3,256,256]{2,1,0:T(8,128)S(1)}, f32[3,256,256]{2,1,0:T(8,128)}, u32[]{:S(2)}, u32[]{:S(2)}) collective-permute-start(f32[3,256,256]{2,1,0:T(8,128)S(1)} %slice.121), channel_id=1, source_target_pairs={{0,4},{4,8},{8,12},{12,16},{16,20},{20,24},{24,28},{28,32},{32,36}... | collective-permute-start | bytes 2359304 | tf_op jit(solution)/shard_map/ppermute | solution.py:15
  1190.8 3.6 copy-start.3
Sparse Core Ops, SparseCore 0:
  18.4 59.9 all-gather.1
  149.8 98.2 all-reduce.3
  529.3 118.8 reduce-scatter.1
  651.5 538.0 all-reduce.5
where the time goes:
time: 1210 us; the launch traced here: 1200 us
  waiting for transfers between devices  807 us (67%)
  local copies, waits for them, and re-layouts  188 us (16%)
  other arithmetic  128 us (11%)
  loops' own time  34.2 us (3%)
  matrix products  22.2 us (2%)
  between operations  14.7 us (1%)
    psum x1, waiting for transfers between devices, shards(): grad_total, weight_total = lax.psum((grad_sum, weight_sum), 'scan')  538 us
    reduce_scatter x1, waiting for transfers between devices, shards(): col_sums = lax.psum_scatter(buffer, 'tile', scatter_dimension=2, tiled=True)  116 us
    psum x1, waiting for transfers between devices, shards(): intensity = lax.psum(local_power, 'tile')  93.4 us
    dynamic_update_slice x16, local copies, waits for them, and re-layouts, accumulate(): lax.dynamic_update_slice(buffer, region + numer, (zero_index, row_at, col...  74.4 us
    all_gather x1, waiting for transfers between devices, shards(): band_all = lax.all_gather(extended, 'tile', axis=2, tiled=True)  54.8 us
    add x16, other arithmetic, accumulate(): return ((buffer, grad_sum + grads, weight_sum + live * weight), None)  35.8 us
    another operation x1, loops' own time, shards(): lax.scan(accumulate, init, (far_re, far_im, factor, windows, live_mask, r...  34 us
    gather x24, local copies, waits for them, and re-layouts  29.4 us
  transfers between devices with their start and end apart: 6, of which 5 were waited for; matrix products, arithmetic and copies ran while one was open for 1% of the time, Pallas kernels for 0%

commit v1 on v0

v1 whole, which is shorter than its diff:
```python
import functools
import math

import jax
import jax.numpy as jnp
import numpy as np
from jax import lax
from jax.experimental import pallas as pl
from jax.experimental.pallas import tpu as pltpu
from jax.sharding import PartitionSpec as P

damping = 1.0
amp_floor = 0.5
MESH = pl.DeviceIdType.MESH
BF = jnp.bfloat16
F32 = jnp.float32


def dft_tables(width):
    index = np.arange(width)
    angle = (index[:, None] * index[None, :] % width) * (2.0 * math.pi / width)
    scale = 1.0 / math.sqrt(width)
    return (np.cos(angle) * scale).astype(BF), (-np.sin(angle) * scale).astype(BF)


def kernel(
    W, XY, NS, NT,
    obj, probe, amp_hbm, cur, prev, fr, fi,
    out_obj, out_probe,
    band_a, band_b, modes, amps, right_f, right_b, left_f, left_b,
    wave, stack, far, near, inten, win, numer, grads, weight, power, illum,
    pass_out, pass_in, total, fwd_out, fwd_in, rs_out, rs_in,
    core_out, core_in, plane_sum, plane_in, z_out, z_in, step_full,
    amp_sem, ag_s, ag_r, fw_s, fw_r, ps_s, ps_r,
    pz_s, pz_r, px_s, px_r, pc_s, pc_r,
    np_s, np_r, nf_s, nf_r, nr_s, nr_r,
    g1_s, g1_r, g2_s, g2_r, g3_s, g3_r, g4_s, g4_r, g5_s, g5_r,
):
    R = W // XY
    s = lax.axis_index("scan")
    t = lax.axis_index("tile")
    core = lax.rem(s, 2)
    zlo = lax.rem(s // 2, 2)
    q = s // 4
    right, left, opp = (lax.rem(t + d, NT) for d in (1, 3, 2))
    other_core = s + 1 - 2 * core
    other_zlo = s + 2 - 4 * zlo
    shard = pl.ds(pl.multiple_of(q * R, R), R)
    has_next = s < NS - 1
    has_prev = s > 0

    def copy_to(src, dst, ssem, rsem, scan, tile):
        return pltpu.make_async_remote_copy(
            src_ref=src, dst_ref=dst, send_sem=ssem, recv_sem=rsem,
            device_id=(scan, tile), device_id_type=MESH,
        )

    def column(step):
        to = lax.rem(q + step, XY)
        return to, to * 4 + zlo * 2 + core

    amp_copies = [
        pltpu.make_async_copy(amp_hbm.at[t + 4 * u], amps.at[u], amp_sem.at[u]) for u in range(2)
    ]
    for item in amp_copies:
        item.start()

    barrier = pltpu.get_barrier_semaphore()

    def greet(scan, tile):
        pl.semaphore_signal(barrier, inc=1, device_id=(scan, tile), device_id_type=MESH)

    for d in range(1, NT):
        greet(s, lax.rem(t + d, NT))
    for d in range(NT):
        greet(other_zlo, lax.rem(t + d, NT))
    greet(other_core, t)

    @pl.loop(1, XY)
    def _(step):
        greet(column(step)[1], t)

    @pl.when(has_next)
    def _():
        greet(s + 1, t)

    @pl.when(has_prev)
    def _():
        greet(s - 1, t)

    band_a[t] = obj[...].astype(BF)
    modes[0] = probe[...].astype(BF)
    pl.semaphore_wait(
        barrier, 2 * NT + XY - 1 + has_next.astype(jnp.int32) + has_prev.astype(jnp.int32)
    )

    to_right = [copy_to(band_a.at[t, p], band_a.at[t, p], ag_s.at[p], ag_r.at[p], s, right) for p in (0, 1)]
    to_left = [copy_to(band_a.at[t, p], band_a.at[t, p], ag_s.at[2 + p], ag_r.at[2 + p], s, left) for p in (0, 1)]
    from_left = [copy_to(band_a.at[left, p], band_a.at[left, p], ag_s.at[p], ag_r.at[p], s, right) for p in (0, 1)]
    from_right = [copy_to(band_a.at[right, p], band_a.at[right, p], ag_s.at[2 + p], ag_r.at[2 + p], s, left) for p in (0, 1)]
    on_right = copy_to(band_a.at[left, 0], band_a.at[left, 0], fw_s.at[0], fw_r.at[0], s, right)
    on_left = copy_to(band_a.at[right, 1], band_a.at[right, 1], fw_s.at[1], fw_r.at[1], s, left)
    opp_first = copy_to(band_a.at[opp, 0], band_a.at[opp, 0], fw_s.at[0], fw_r.at[0], s, right)
    opp_second = copy_to(band_a.at[opp, 1], band_a.at[opp, 1], fw_s.at[1], fw_r.at[1], s, left)

    def passed(block, slot):
        return copy_to(band_a.at[block], band_b.at[block], ps_s.at[slot], ps_r.at[slot], s - 1, t)

    def start_pass(block, slot):
        @pl.when(has_prev)
        def _():
            passed(block, slot).start()

    to_right[0].start()
    to_left[1].start()
    to_right[1].start()
    to_left[0].start()
    start_pass(t, 0)

    for d in range(1, NT):
        copy_to(
            modes.at[0, core, :, shard], modes.at[NT - d, core, :, shard],
            pz_s.at[d], pz_r.at[NT - d], s, lax.rem(t + d, NT),
        ).start()
    for d in range(1, NT):
        copy_to(
            modes.at[0, core, :, shard], modes.at[d, core, :, shard], pz_s.at[d], pz_r.at[d], s, t
        ).wait_recv()

    def over_columns(step):
        to, device = column(step)
        src = modes.at[pl.ds(1, NT - 1), core, :, shard]
        return copy_to(src, src, px_s.at[to], px_r.at[q], device, t)

    @pl.loop(1, XY)
    def _(step):
        over_columns(step).start()

    from_left[0].wait_recv()
    on_right.start()
    from_right[1].wait_recv()
    on_left.start()
    from_left[1].wait_recv()
    start_pass(left, 1)
    from_right[0].wait_recv()
    start_pass(right, 2)

    for table, ref in ((1.0, right_f), (-1.0, right_b)):
        sign = jnp.asarray(table, BF)
        ref[0:W, 0:W] = fr[...]
        ref[0:W, W:] = fi[...] * sign
        ref[W:, 0:W] = fi[...] * -sign
        ref[W:, W:] = fr[...]
    left_f[:, 0:W] = fr[...]
    left_f[:, W:] = -fi[...]
    left_b[:, 0:W] = fr[...]
    left_b[:, W:] = fi[...]

    opp_first.wait_recv()
    opp_second.wait_recv()
    start_pass(opp, 3)

    @pl.loop(1, XY)
    def _(step):
        source = lax.rem(q + step, XY)
        rows = pl.ds(pl.multiple_of(source * R, R), R)
        dst = modes.at[pl.ds(1, NT - 1), core, :, rows]
        copy_to(dst, dst, px_s.at[source], px_r.at[source], s, right).wait_recv()

    to_core = copy_to(
        modes.at[pl.ds(1, NT - 1), core], modes.at[pl.ds(1, NT - 1), core], pc_s, pc_r, other_core, t
    )
    from_core = copy_to(
        modes.at[pl.ds(1, NT - 1), 1 - core], modes.at[pl.ds(1, NT - 1), 1 - core], pc_s, pc_r, other_core, t
    )
    to_core.start()

    @pl.when(has_next)
    def _():
        for slot, block in enumerate((t, left, right, opp)):
            copy_to(band_a.at[block], band_b.at[block], ps_s.at[slot], ps_r.at[slot], s + 1, t).wait_recv()

    from_core.wait_recv()
    for item in amp_copies:
        item.wait()

    row_id = lax.broadcasted_iota(jnp.int32, (W, W), 0)
    col_id = lax.broadcasted_iota(jnp.int32, (W, W), 1)

    def place(table, slot, first):
        row = table[2 * slot] - first
        col = table[2 * slot + 1]
        live = jnp.where(slot < table[16], 1.0, 0.0).astype(F32)
        return row, lax.rem(col, W), col // W, live

    C = min(32, W)

    def by_rows(body):
        @pl.loop(0, W // C)
        def _(step):
            body(pl.ds(pl.multiple_of(step * C, C), C))

    def transform(right_table, left_table):
        half = jnp.dot(wave[...], right_table[...], preferred_element_type=F32).astype(BF)
        stack[0:W, :] = half
        stack[W:, 0:W] = half[:, W:]
        stack[W:, W:] = -half[:, 0:W]
        return jnp.dot(left_table[...], stack[...], preferred_element_type=F32)

    for u in range(2):
        row, lane, block, live = place(cur, t + 4 * u, s * W)
        after = jnp.minimum(block + 1, NT - 1)
        for p in range(2):
            upper = jnp.where(col_id >= lane, band_a[block, p].astype(F32), band_a[after, p].astype(F32))
            lower = jnp.where(col_id >= lane, band_b[block, p].astype(F32), band_b[after, p].astype(F32))
            merged = jnp.where(row_id >= row, upper, lower)
            merged = pltpu.roll(merged, lax.rem(W - row, W), 0)
            win[p] = pltpu.roll(merged, lax.rem(W - lane, W), 1)

        def start_slot(rows):
            square = live * (win[0, rows] * win[0, rows] + win[1, rows] * win[1, rows])
            weight[rows] = square if u == 0 else weight[rows] + square
            inten[rows] = jnp.zeros((C, W), F32)
            for p in range(2):
                numer[u, p, rows] = jnp.zeros((C, W), F32)

        by_rows(start_slot)

        @pl.loop(0, 2 * NT)
        def _(m):
            i, cc = m // 2, lax.rem(m, 2)

            def exit_rows(rows):
                pr = modes[i, cc, 0, rows].astype(F32)
                pi = modes[i, cc, 1, rows].astype(F32)
                wr, wi = win[0, rows], win[1, rows]
                wave[rows, 0:W] = (pr * wr - pi * wi).astype(BF)
                wave[rows, W:] = (pr * wi + pi * wr).astype(BF)
                if u == 0:
                    square = pr * pr + pi * pi
                    power[rows] = jnp.where(m == 0, 0.0, power[rows]) + square

            by_rows(exit_rows)
            far[m] = transform(right_f, left_f)

            def add_rows(rows):
                fa, fb = far[m, rows, 0:W], far[m, rows, W:]
                inten[rows] += fa * fa + fb * fb

            by_rows(add_rows)

        def factor_rows(rows):
            size = jnp.maximum(jnp.sqrt(inten[rows]), amp_floor)
            inten[rows] = live * (amps[u, rows].astype(F32) / size - 1.0)

        by_rows(factor_rows)

        @pl.loop(0, 2 * NT)
        def _(m):
            i, cc = m // 2, lax.rem(m, 2)

            def change_rows(rows):
                factor = inten[rows]
                wave[rows, 0:W] = (factor * far[m, rows, 0:W]).astype(BF)
                wave[rows, W:] = (factor * far[m, rows, W:]).astype(BF)

            by_rows(change_rows)
            near[...] = transform(right_b, left_b)

            def near_rows(rows):
                pr = modes[i, cc, 0, rows].astype(F32)
                pi = modes[i, cc, 1, rows].astype(F32)
                wr, wi = win[0, rows], win[1, rows]
                nr, ni = near[rows, 0:W], near[rows, W:]
                numer[u, 0, rows] += pr * nr + pi * ni
                numer[u, 1, rows] += pr * ni - pi * nr
                gr = wr * nr + wi * ni
                gi = wr * ni - wi * nr
                grads[i, cc, 0, rows] = gr if u == 0 else grads[i, cc, 0, rows] + gr
                grads[i, cc, 1, rows] = gi if u == 0 else grads[i, cc, 1, rows] + gi

            by_rows(near_rows)

        for p in range(2):
            rolled = pltpu.roll(numer[u, p], lane, 1)
            numer[u, p] = pltpu.roll(rolled, row, 0)

    def core_rows(rows):
        for i in range(NT):
            for p in range(2):
                core_out[2 * i + p, rows] = grads[i, 1 - core, p, rows].astype(BF)
        core_out[2 * NT, rows] = weight[rows].astype(BF)

    by_rows(core_rows)
    g1 = copy_to(core_out, core_in, g1_s, g1_r, other_core, t)
    g1.start()

    spots = [place(cur, t + 4 * u, s * W) for u in range(2)]

    def band_part(block, p, upper):
        value = 0.0
        for u, (row, lane, first, _) in enumerate(spots):
            cols = jnp.where(col_id >= lane, first, first + 1) == block
            rows = (row_id >= row) if upper else (row_id < row)
            value = value + jnp.where(cols & rows, numer[u, p], 0.0)
        return value

    def pass_sum(slot):
        return copy_to(pass_out.at[slot], pass_in.at[slot], np_s.at[slot], np_r.at[slot], s + 1, t)

    order = (opp, right, left, t)
    for slot, block in enumerate(order):
        for p in range(2):
            pass_out[slot, p] = band_part(block, p, False).astype(BF)

        @pl.when(has_next)
        def _():
            pass_sum(slot).start()

    g1.wait_recv()

    def sum_rows(rows):
        for i in range(NT):
            for p in range(2):
                k = 2 * i + p
                plane_sum[k, rows] = (grads[i, core, p, rows] + core_in[k, rows].astype(F32)).astype(BF)
        plane_sum[2 * NT, rows] = (weight[rows] + core_in[2 * NT, rows].astype(F32)).astype(BF)

    by_rows(sum_rows)

    def g2(step):
        to, device = column(step)
        rows = pl.ds(pl.multiple_of(to * R, R), R)
        return copy_to(plane_sum.at[:, rows], plane_in.at[q], g2_s.at[to], g2_r.at[q], device, t)

    @pl.loop(1, XY)
    def _(step):
        g2(step).start()

    for slot, block in enumerate(order):
        for p in range(2):
            total[slot, p] = band_part(block, p, True)

    illum[...] = jnp.zeros((W, W), F32)
    for table, first, upper in ((cur, s * W, True), (prev, (s - 1) * W, False)):
        @pl.loop(0, 8)
        def _(slot):
            row, lane, block, live = place(table, slot, first)
            row = lax.rem(row + W, W)
            moved = pltpu.roll(pltpu.roll(power[...], lane, 1), row, 0)
            cols = jnp.where(col_id >= lane, block, block + 1) == t
            rows = (row_id >= row) if upper else (row_id < row)
            illum[...] += live * jnp.where(cols & rows, moved, 0.0)

    def take_pass(slot):
        @pl.when(has_prev)
        def _():
            copy_to(pass_out.at[slot], pass_in.at[slot], np_s.at[slot], np_r.at[slot], s - 1, t).wait_recv()
            for p in range(2):
                total[slot, p] += pass_in[slot, p].astype(F32)

    take_pass(0)
    forwards = []
    for p, to in ((0, right), (1, left)):
        fwd_out[p] = total[0, p].astype(BF)
        item = copy_to(fwd_out.at[p], fwd_in.at[p], nf_s.at[p], nf_r.at[p], s, to)
        item.start()
        forwards.append(item)
    sends = {}
    for way, to in ((0, right), (1, left)):
        for p in range(2):
            sends[way, p] = copy_to(
                rs_out.at[way, p], rs_in.at[way, p], nr_s.at[way, p], nr_r.at[way, p], s, to
            )
    take_pass(1)
    rs_out[0, 1] = total[1, 1].astype(BF)
    sends[0, 1].start()
    take_pass(2)
    rs_out[1, 0] = total[2, 0].astype(BF)
    sends[1, 0].start()
    forwards[0].wait_recv()
    rs_out[0, 0] = (total[1, 0] + fwd_in[0].astype(F32)).astype(BF)
    sends[0, 0].start()
    forwards[1].wait_recv()
    rs_out[1, 1] = (total[2, 1] + fwd_in[1].astype(F32)).astype(BF)
    sends[1, 1].start()

    @pl.loop(1, XY)
    def _(step):
        source = lax.rem(q + step, XY)
        copy_to(plane_sum.at[:, shard], plane_in.at[source], g2_s.at[source], g2_r.at[source], s, right).wait_recv()

    plane_in[q] = plane_sum[:, shard]
    for k in range(2 * NT + 1):
        value = plane_in[0, k].astype(F32)
        for source in range(1, XY):
            value = value + plane_in[source, k].astype(F32)
        if k < 2 * NT:
            z_out[k // 2, k % 2] = value
        else:
            for i in range(NT):
                z_out[i, 2] = value
    me_z = 2 * t + zlo
    z_in[me_z] = z_out[0]
    z_copies = []
    for flip in range(2):
        for d in range(NT):
            if flip == 0 and d == 0:
                continue
            k = flip * NT + d
            scan = other_zlo if flip else s
            item = copy_to(z_out.at[d], z_in.at[me_z], g3_s.at[k], g3_r.at[me_z], scan, lax.rem(t + d, NT))
            item.start()
            z_copies.append(item)

    take_pass(3)
    for item in sends.values():
        item.wait_recv()
    for p in range(2):
        value = total[3, p] + (rs_in[0, p].astype(F32) + rs_in[1, p].astype(F32))
        out_obj[p] = obj[p] + value / (illum[...] + damping)

    for flip in range(2):
        for d in range(NT):
            if flip == 0 and d == 0:
                continue
            source = 2 * lax.rem(t + d, NT) + (1 - zlo if flip else zlo)
            copy_to(z_out.at[d], z_in.at[source], g3_s.at[d], g3_r.at[source], s, right).wait_recv()
    summed = [z_in[0, k] for k in range(3)]
    for source in range(1, 2 * NT):
        summed = [summed[k] + z_in[source, k] for k in range(3)]
    for p in range(2):
        step_full[core, p, shard] = summed[p] / (summed[2] + damping)

    def g4(step):
        to, device = column(step)
        src = step_full.at[core, :, shard]
        return copy_to(src, src, g4_s.at[to], g4_r.at[q], device, t)

    @pl.loop(1, XY)
    def _(step):
        g4(step).start()

    @pl.loop(1, XY)
    def _(step):
        source = lax.rem(q + step, XY)
        rows = pl.ds(pl.multiple_of(source * R, R), R)
        dst = step_full.at[core, :, rows]
        copy_to(dst, dst, g4_s.at[source], g4_r.at[source], s, right).wait_recv()

    g5 = copy_to(step_full.at[core], step_full.at[core], g5_s, g5_r, other_core, t)
    g5.start()
    copy_to(step_full.at[1 - core], step_full.at[1 - core], g5_s, g5_r, other_core, t).wait_recv()
    out_probe[...] = step_full[...]

    for item in to_right + to_left + [on_right, on_left, to_core, g1, g5] + forwards + z_copies + list(sends.values()):
        item.wait_send()
    for d in range(1, NT):
        copy_to(
            modes.at[0, core, :, shard], modes.at[NT - d, core, :, shard],
            pz_s.at[d], pz_r.at[NT - d], s, lax.rem(t + d, NT),
        ).wait_send()

    @pl.loop(1, XY)
    def _(step):
        over_columns(step).wait_send()
        g2(step).wait_send()
        g4(step).wait_send()

    @pl.when(has_prev)
    def _():
        for slot, block in enumerate((t, left, right, opp)):
            passed(block, slot).wait_send()

    @pl.when(has_next)
    def _():
        for slot in range(NT):
            pass_sum(slot).wait_send()


def shards(NS, NT, object_field, probe_modes, amplitudes, positions, counts):
    W = amplitudes.shape[1]
    XY = NS // 4
    R = W // XY
    fr, fi = dft_tables(W)
    table = jnp.concatenate([positions.reshape(-1), counts])
    before = lax.ppermute(table, "scan", [(k, k + 1) for k in range(NS - 1)])
    vmem = pl.BlockSpec(memory_space=pltpu.VMEM)
    smem = pl.BlockSpec(memory_space=pltpu.SMEM)
    dma = pltpu.SemaphoreType.DMA

    def buf(*shape, dtype=F32):
        return pltpu.VMEM(shape, dtype)

    scratch = [
        buf(NT, 2, W, W, dtype=BF), buf(NT, 2, W, W, dtype=BF), buf(NT, 2, 2, W, W, dtype=BF),
        buf(2, W, W, dtype=BF), buf(2 * W, 2 * W, dtype=BF), buf(2 * W, 2 * W, dtype=BF),
        buf(W, 2 * W, dtype=BF), buf(W, 2 * W, dtype=BF),
        buf(W, 2 * W, dtype=BF), buf(2 * W, 2 * W, dtype=BF), buf(2 * NT, W, 2 * W), buf(W, 2 * W),
        buf(W, W), buf(2, W, W), buf(2, 2, W, W), buf(NT, 2, 2, W, W), buf(W, W), buf(W, W), buf(W, W),
        buf(NT, 2, W, W, dtype=BF), buf(NT, 2, W, W, dtype=BF), buf(NT, 2, W, W),
        buf(2, W, W, dtype=BF), buf(2, W, W, dtype=BF), buf(2, 2, W, W, dtype=BF), buf(2, 2, W, W, dtype=BF),
        buf(2 * NT + 1, W, W, dtype=BF), buf(2 * NT + 1, W, W, dtype=BF), buf(2 * NT + 1, W, W, dtype=BF),
        buf(XY, 2 * NT + 1, R, W, dtype=BF), buf(NT, 3, R, W), buf(2 * NT, 3, R, W), buf(2, 2, W, W),
        dma((2,)), dma((4,)), dma((4,)), dma((2,)), dma((2,)), dma((4,)), dma((4,)),
        dma((NT,)), dma((NT,)), dma((XY,)), dma((XY,)), dma, dma,
        dma((NT,)), dma((NT,)), dma((2,)), dma((2,)), dma((2, 2)), dma((2, 2)),
        dma, dma, dma((XY,)), dma((XY,)), dma((2 * NT,)), dma((2 * NT,)), dma((XY,)), dma((XY,)), dma, dma,
    ]
    new_object, probe_step = pl.pallas_call(
        functools.partial(kernel, W, XY, NS, NT),
        out_shape=(
            jax.ShapeDtypeStruct(object_field.shape, F32),
            jax.ShapeDtypeStruct(probe_modes.shape, F32),
        ),
        in_specs=[vmem, vmem, pl.BlockSpec(memory_space=pl.ANY), smem, smem, vmem, vmem],
        out_specs=(vmem, vmem),
        scratch_shapes=scratch,
        compiler_params=pltpu.CompilerParams(
            collective_id=0, has_side_effects=True, vmem_limit_bytes=58 * 1024 * 1024
        ),
    )(object_field, probe_modes, amplitudes, table, before, jnp.asarray(fr), jnp.asarray(fi))
    return new_object, probe_step


def solution(mesh):
    placed = (
        P(None, "scan", "tile"),
        P("tile", None, None, None),
        P("scan", None, None),
        P("scan", None),
        P("scan"),
    )
    return jax.shard_map(
        functools.partial(shards, mesh.shape["scan"], mesh.shape["tile"]),
        mesh=mesh,
        in_specs=placed,
        out_specs=(P(None, "scan", "tile"), P("tile", None, None, None)),
        check_vma=False,
    )
```

time: 1210 us -> 142 us (0.12)
  waiting for transfers between devices: 807 us -> 0.7 us
  local copies, waits for them, and re-layouts: 188 us -> 3.62 us
  Pallas kernels: 0 us -> 131 us
  other arithmetic: 128 us -> 0.08 us
  loops' own time: 34.2 us -> 0 us
  matrix products: 22.2 us -> 0 us
  between operations: 14.7 us -> 1.33 us
    psum x2 -> x0, waiting for transfers between devices: 632 us -> none  [the longest x1 538 us: shards(): grad_total, weight_total = lax.psum((grad_sum, weight_sum), 'scan')]
    pallas_call x0 -> x1, Pallas kernels: none -> 131 us  [shards(): pl.pallas_call(functools.partial(kernel, W, XY, NS, NT), out_shape=(jax.S...]
    reduce_scatter x1 -> x0, waiting for transfers between devices: 116 us -> none  [shards(): col_sums = lax.psum_scatter(buffer, 'tile', scatter_dimension=2, tiled=True)]
    dynamic_update_slice x32 -> x0, local copies, waits for them, and re-layouts: 81.2 us -> none  [the longest x16 74.4 us: accumulate(): lax.dynamic_update_slice(buffer, region + numer, (zero_index, row_at, col...]
    all_gather x1 -> x0, waiting for transfers between devices: 54.8 us -> none  [shards(): band_all = lax.all_gather(extended, 'tile', axis=2, tiled=True)]
    dynamic_slice x64 -> x0, local copies, waits for them, and re-layouts: 44.1 us -> none  [the longest x48 29.3 us: shards(): lax.scan(accumulate, init, (far_re, far_im, factor, windows, live_mask, r...]
    add x27 -> x0, other arithmetic: 39.7 us -> none  [the longest x16 35.8 us: accumulate(): return ((buffer, grad_sum + grads, weight_sum + live * weight), None)]
    another operation x3 -> x0, loops' own time: 34.2 us -> none  [the longest x1 34 us: shards(): lax.scan(accumulate, init, (far_re, far_im, factor, windows, live_mask, r...]
  transfers between devices with their start and end apart: 6 -> 1, of which waited for: 5 -> 1; matrix products, arithmetic and copies ran while one was open for 1% -> 0% of each run, Pallas kernels for 0% -> 0%
where the time goes in v1:
time: 142 us
  Pallas kernels  131 us (92%)
  starting transfers between devices  4.93 us (3%)
  local copies, waits for them, and re-layouts  3.62 us (3%)
    pallas_call x1, Pallas kernels, shards(): pl.pallas_call(functools.partial(kernel, W, XY, NS, NT), out_shape=(jax.S...  131 us
    ppermute x1, starting transfers between devices, shards(): before = lax.ppermute(table, 'scan', [(k, k + 1) for k in range(NS - 1)])  4.93 us
    unnamed x11, local copies, waits for them, and re-layouts  3.54 us
  transfers between devices with their start and end apart: 1, of which 1 were waited for; matrix products, arithmetic and copies ran while one was open for 0% of the time, Pallas kernels for 0%

profile of v1, /device:TPU:1, one launch (start us, length us, event | category | flops | bytes accessed | tf_op | source)
XLA Modules:
  0.0 141.9 jit_solution(15106303028252168300)
XLA Ops:
  0.6 0.0 copy-start.1
  1.3 0.0 copy-done.1
  1.3 0.1 copy.10
  1.4 0.1 reshape.7
  1.5 0.1 pad_add_fusion.cur
  1.6 0.0 copy-start.2
  1.6 4.9 %collective-permute-start = (s32[17]{0:T(128)S(1)}, s32[17]{0:T(128)S(1)}, u32[]{:S(2)}, u32[]{:S(2)}) collective-permute-start(s32[17]{0:T(128)S(1)} %pad_add_fusion.cur), channel_id=1, source_target_pairs={{0,4},{4,8},{8,12},{12,16},{16,20},{20,24},{24,28},{28,32},{32,36}... | collective-permute-start | bytes 212 | tf_op jit(solution)/shard_map/ppermute | solution.py:487
  6.5 0.7 collective-permute-done.prev
  7.2 0.0 copy-done.2
  7.2 0.0 copy-start.3
  7.2 0.5 copy-done.3
  7.7 131.2 %shard_map.86 = (f32[2,256,256]{2,1,0:T(8,128)}, f32[2,2,256,256]{3,2,1,0:T(8,128)}) custom-call(f32[2,256,256]{2,1,0:T(8,128)} %obj.1, f32[2,2,256,256]{3,2,1,0:T(8,128)} %probe.1, bf16[8,256,256]{2,1,0:T(8,128)(2,1)} %amp_hbm.1, s32[17]{0:T(128)} %copy-done.2, s32[17]{0:T(128)} %copy-done.3, bf16[256,256]{1,0:T(8,128)(2,1)} %constant.4.clone.fr, ...), custom_call_target="tpu_custom_call" | custom-call | tf_op jit(solution)/shard_map/pallas_call | solution.py:510
  138.9 0.0 copy-start
  138.9 2.0 %copy.14 = f32[2,256,256]{2,1,0:T(8,128)} copy(f32[2,256,256]{2,1,0:T(8,128)} %get-tuple-element.4) | data formatting | bytes 1048576
  140.9 0.0 copy-done
  140.9 1.0 copy.15
Async XLA Ops:
  0.6 0.7 copy-start.1
  1.6 5.6 %copy-start.2 = (s32[17]{0:T(128)}, s32[17]{0:T(128)S(1)}, u32[]{:S(2)}) copy-start(s32[17]{0:T(128)S(1)} %pad_add_fusion.cur) | copy-start | bytes 208
  1.6 5.6 %collective-permute-start = (s32[17]{0:T(128)S(1)}, s32[17]{0:T(128)S(1)}, u32[]{:S(2)}, u32[]{:S(2)}) collective-permute-start(s32[17]{0:T(128)S(1)} %pad_add_fusion.cur), channel_id=1, source_target_pairs={{0,4},{4,8},{8,12},{12,16},{16,20},{20,24},{24,28},{28,32},{32,36}... | collective-permute-start | bytes 212 | tf_op jit(solution)/shard_map/ppermute | solution.py:487
  7.2 0.5 copy-start.3
  138.9 2.0 %copy-start = (f32[2,2,256,256]{3,2,1,0:T(8,128)S(1)}, f32[2,2,256,256]{3,2,1,0:T(8,128)}, u32[]{:S(2)}) copy-start(f32[2,2,256,256]{3,2,1,0:T(8,128)} %get-tuple-element.5) | copy-start | bytes 3145732

commit v2 on v1

v2 whole, which is shorter than its diff:
```python
import functools
import math

import jax
import jax.numpy as jnp
import numpy as np
from jax import lax
from jax.experimental import pallas as pl
from jax.experimental.pallas import tpu as pltpu
from jax.sharding import PartitionSpec as P

damping = 1.0
amp_floor = 0.5
MESH = pl.DeviceIdType.MESH
BF = jnp.bfloat16
F32 = jnp.float32


def dft_tables(width):
    index = np.arange(width)
    angle = (index[:, None] * index[None, :] % width) * (2.0 * math.pi / width)
    scale = 1.0 / math.sqrt(width)
    return (np.cos(angle) * scale).astype(BF), (-np.sin(angle) * scale).astype(BF)


def kernel(
    W, XY, NS, NT,
    obj_hbm, probe_hbm, amp_hbm, pos, cnt, pos_hbm, cnt_hbm, fr, fi,
    out_obj, out_probe,
    obj, probe, band_a, band_b, modes, amps, right_f, right_b, left_f, left_b,
    wave, stack, far, near, inten, win, numer, grads, weight, power, illum,
    pos_land, cnt_land, prev_pos, prev_cnt,
    pass_out, pass_in, total, fwd_out, fwd_in, rs_out, rs_in,
    core_out, core_in, plane_sum, plane_in, z_out, z_in, step_full,
    in_sem, sm_sem, tb_s, tb_r, ag_s, ag_r, fw_s, fw_r, ps_s, ps_r,
    pz_s, pz_r, px_s, px_r, pc_s, pc_r,
    np_s, np_r, nf_s, nf_r, nr_s, nr_r,
    g1_s, g1_r, g2_s, g2_r, gw_s, gw_r, g3_s, g3_r, g4_s, g4_r, g5_s, g5_r,
):
    R = W // XY
    C = min(32, W)
    s = lax.axis_index("scan")
    t = lax.axis_index("tile")
    core = lax.rem(s, 2)
    zlo = lax.rem(s // 2, 2)
    q = s // 4
    right, left, opp = (lax.rem(t + d, NT) for d in (1, 3, 2))
    other_core = s + 1 - 2 * core
    other_zlo = s + 2 - 4 * zlo
    shard = pl.ds(pl.multiple_of(q * R, R), R)
    has_next = s < NS - 1
    has_prev = s > 0

    def copy_to(src, dst, ssem, rsem, scan, tile):
        return pltpu.make_async_remote_copy(
            src_ref=src, dst_ref=dst, send_sem=ssem, recv_sem=rsem,
            device_id=(scan, tile), device_id_type=MESH,
        )

    def column(step):
        to = lax.rem(q + step, XY)
        return to, to * 4 + zlo * 2 + core

    def by_rows(body):
        @pl.loop(0, W // C)
        def _(step):
            body(pl.ds(pl.multiple_of(step * C, C), C))

    local = [
        pltpu.make_async_copy(src, dst, in_sem.at[k])
        for k, (src, dst) in enumerate((
            (obj_hbm, obj), (probe_hbm, probe), (amp_hbm.at[t], amps.at[0]), (amp_hbm.at[t + 4], amps.at[1]),
        ))
    ]
    for item in local:
        item.start()

    barrier = pltpu.get_barrier_semaphore()

    def greet(scan, tile):
        pl.semaphore_signal(barrier, inc=1, device_id=(scan, tile), device_id_type=MESH)

    for d in range(1, NT):
        greet(s, lax.rem(t + d, NT))
    for d in range(NT):
        greet(other_zlo, lax.rem(t + d, NT))
    greet(other_core, t)

    @pl.loop(1, XY)
    def _(step):
        greet(column(step)[1], t)

    up_tile = lax.rem(t + jnp.where((core == 0) & (zlo == 1), 1, 0) + jnp.where((core == 0) & (zlo == 0), NT - 1, 0), NT)
    up_tile = jnp.where((core == 0), up_tile, t)
    down_tile = lax.rem(t + jnp.where((core == 1) & (zlo == 0), NT - 1, 0) + jnp.where((core == 1) & (zlo == 1), 1, 0), NT)

    @pl.when(has_next)
    def _():
        greet(s + 1, t)
        greet(s + 1, down_tile)

    @pl.when(has_prev)
    def _():
        greet(s - 1, t)
        greet(s - 1, up_tile)

    local[1].wait()
    modes[0] = probe[...].astype(BF)
    local[0].wait()
    band_a[t] = obj[...].astype(BF)
    pl.semaphore_wait(
        barrier, 2 * NT + XY - 1 + 2 * has_next.astype(jnp.int32) + 2 * has_prev.astype(jnp.int32)
    )

    for d in range(1, NT):
        copy_to(
            modes.at[0, core, :, shard], modes.at[NT - d, core, :, shard],
            pz_s.at[d], pz_r.at[NT - d], s, lax.rem(t + d, NT),
        ).start()

    to_right = [copy_to(band_a.at[t, p], band_a.at[t, p], ag_s.at[p], ag_r.at[p], s, right) for p in (0, 1)]
    to_left = [copy_to(band_a.at[t, p], band_a.at[t, p], ag_s.at[2 + p], ag_r.at[2 + p], s, left) for p in (0, 1)]
    from_left = [copy_to(band_a.at[left, p], band_a.at[left, p], ag_s.at[p], ag_r.at[p], s, right) for p in (0, 1)]
    from_right = [copy_to(band_a.at[right, p], band_a.at[right, p], ag_s.at[2 + p], ag_r.at[2 + p], s, left) for p in (0, 1)]
    on_right = copy_to(band_a.at[left, 0], band_a.at[left, 0], fw_s.at[0], fw_r.at[0], s, right)
    on_left = copy_to(band_a.at[right, 1], band_a.at[right, 1], fw_s.at[1], fw_r.at[1], s, left)
    opp_first = copy_to(band_a.at[opp, 0], band_a.at[opp, 0], fw_s.at[0], fw_r.at[0], s, right)
    opp_second = copy_to(band_a.at[opp, 1], band_a.at[opp, 1], fw_s.at[1], fw_r.at[1], s, left)

    def passed(block, p):
        return copy_to(
            band_a.at[block, p], band_b.at[block, p], ps_s.at[block, p], ps_r.at[block, p],
            s - 1, up_tile if p == 0 else t,
        )

    def start_pass(block, *planes):
        @pl.when(has_prev)
        def _():
            for p in planes:
                passed(block, p).start()

    to_right[0].start()
    to_left[1].start()
    to_right[1].start()
    to_left[0].start()
    start_pass(t, 0, 1)

    tables = [
        copy_to(src, dst, tb_s.at[k], tb_r.at[k], s + 1, t)
        for k, (src, dst) in enumerate(((pos_hbm, pos_land), (cnt_hbm, cnt_land)))
    ]

    @pl.when(has_next)
    def _():
        for item in tables:
            item.start()

    for d in range(1, NT):
        copy_to(
            modes.at[0, core, :, shard], modes.at[d, core, :, shard], pz_s.at[d], pz_r.at[d], s, t
        ).wait_recv()

    def over_columns(step):
        to, device = column(step)
        src = modes.at[pl.ds(1, NT - 1), core, :, shard]
        return copy_to(src, src, px_s.at[to], px_r.at[q], device, t)

    @pl.loop(1, XY)
    def _(step):
        over_columns(step).start()

    from_left[0].wait_recv()
    on_right.start()
    from_right[1].wait_recv()
    on_left.start()
    start_pass(left, 0)
    start_pass(right, 1)
    from_left[1].wait_recv()
    start_pass(left, 1)
    from_right[0].wait_recv()
    start_pass(right, 0)

    for table, ref in ((1.0, right_f), (-1.0, right_b)):
        sign = jnp.asarray(table, BF)
        ref[0:W, 0:W] = fr[...]
        ref[0:W, W:] = fi[...] * sign
        ref[W:, 0:W] = fi[...] * -sign
        ref[W:, W:] = fr[...]
    left_f[:, 0:W] = fr[...]
    left_f[:, W:] = -fi[...]
    left_b[:, 0:W] = fr[...]
    left_b[:, W:] = fi[...]

    opp_first.wait_recv()
    start_pass(opp, 0)
    opp_second.wait_recv()
    start_pass(opp, 1)

    @pl.loop(1, XY)
    def _(step):
        source = lax.rem(q + step, XY)
        rows = pl.ds(pl.multiple_of(source * R, R), R)
        dst = modes.at[pl.ds(1, NT - 1), core, :, rows]
        copy_to(dst, dst, px_s.at[source], px_r.at[source], s, right).wait_recv()

    def to_core(i):
        return copy_to(modes.at[i, core], modes.at[i, core], pc_s.at[i], pc_r.at[i], other_core, t)

    for i in range(1, NT):
        to_core(i).start()

    prev_copies = [
        pltpu.make_async_copy(src, dst, sm_sem.at[k])
        for k, (src, dst) in enumerate(((pos_land, prev_pos), (cnt_land, prev_cnt)))
    ]

    @pl.when(has_prev)
    def _():
        for item, copy in zip(tables, prev_copies):
            item.wait_recv()
            copy.start()

    for item in local[2:]:
        item.wait()

    @pl.when(has_next)
    def _():
        for block in (t, left, right, opp):
            for p in range(2):
                copy_to(
                    band_a.at[block, p], band_b.at[block, p], ps_s.at[block, p], ps_r.at[block, p], s + 1, t
                ).wait_recv()

    row_id = lax.broadcasted_iota(jnp.int32, (W, W), 0)
    col_id = lax.broadcasted_iota(jnp.int32, (W, W), 1)

    def place(slot):
        row, col = pos[slot, 0] - s * W, pos[slot, 1]
        live = jnp.where(slot < cnt[0], 1.0, 0.0).astype(F32)
        return row, lax.rem(col, W), col // W, live

    def place_prev(slot):
        row = jnp.where(has_prev, prev_pos[slot, 0] - (s - 1) * W, 0)
        col = jnp.where(has_prev, prev_pos[slot, 1], 0)
        live = jnp.where(has_prev & (slot < prev_cnt[0]), 1.0, 0.0).astype(F32)
        return row, lax.rem(col, W), col // W, live

    def transform(right_table, left_table):
        half = jnp.dot(wave[...], right_table[...], preferred_element_type=F32).astype(BF)
        stack[0:W, :] = half
        stack[W:, 0:W] = half[:, W:]
        stack[W:, W:] = -half[:, 0:W]
        return jnp.dot(left_table[...], stack[...], preferred_element_type=F32)

    def pass_sum(u):
        return copy_to(pass_out.at[u], pass_in.at[u], np_s.at[u], np_r.at[u], s + 1, t)

    last = 2 * NT

    def g1(i):
        planes = pl.ds(2 * i, 2)
        return copy_to(core_out.at[planes], core_in.at[planes], g1_s.at[i], g1_r.at[i], other_core, t)

    g1w = copy_to(core_out.at[last], core_in.at[last], g1_s.at[NT], g1_r.at[NT], other_core, t)

    def shard_of(to):
        return pl.ds(pl.multiple_of(to * R, R), R)

    def g2(i, step):
        to, device = column(step)
        planes = pl.ds(2 * i, 2)
        return copy_to(
            plane_sum.at[planes, shard_of(to)], plane_in.at[q, planes], g2_s.at[i, to], g2_r.at[i, q], device, t
        )

    def g2w(step):
        to, device = column(step)
        return copy_to(plane_sum.at[last, shard_of(to)], plane_in.at[q, last], gw_s.at[to], gw_r.at[q], device, t)

    for u in range(2):
        row, lane, block, live = place(t + 4 * u)
        after = jnp.minimum(block + 1, NT - 1)
        for p in range(2):
            upper = jnp.where(col_id >= lane, band_a[block, p].astype(F32), band_a[after, p].astype(F32))
            lower = jnp.where(col_id >= lane, band_b[block, p].astype(F32), band_b[after, p].astype(F32))
            merged = jnp.where(row_id >= row, upper, lower)
            merged = pltpu.roll(merged, lax.rem(W - row, W), 0)
            win[p] = pltpu.roll(merged, lax.rem(W - lane, W), 1)

        def start_slot(rows):
            square = live * (win[0, rows] * win[0, rows] + win[1, rows] * win[1, rows])
            if u == 0:
                weight[rows] = square
            else:
                weight[rows] += square
                core_out[last, rows] = weight[rows].astype(BF)
            inten[rows] = jnp.zeros((C, W), F32)
            for p in range(2):
                numer[u, p, rows] = jnp.zeros((C, W), F32)

        by_rows(start_slot)
        if u == 1:
            g1w.start()

        @pl.loop(0, 2 * NT)
        def _(m):
            i, cc = m // 2, lax.rem(m, 2)
            if u == 0:
                @pl.when((i > 0) & (cc == 0))
                def _():
                    copy_to(modes.at[i, 1 - core], modes.at[i, 1 - core], pc_s.at[i], pc_r.at[i], other_core, t).wait_recv()

            def exit_rows(rows):
                pr = modes[i, cc, 0, rows].astype(F32)
                pi = modes[i, cc, 1, rows].astype(F32)
                wr, wi = win[0, rows], win[1, rows]
                wave[rows, 0:W] = (pr * wr - pi * wi).astype(BF)
                wave[rows, W:] = (pr * wi + pi * wr).astype(BF)
                if u == 0:
                    square = pr * pr + pi * pi
                    power[rows] = jnp.where(m == 0, 0.0, power[rows]) + square

            by_rows(exit_rows)
            far[m] = transform(right_f, left_f)

            def add_rows(rows):
                fa, fb = far[m, rows, 0:W], far[m, rows, W:]
                inten[rows] += fa * fa + fb * fb

            by_rows(add_rows)

        def factor_rows(rows):
            size = jnp.maximum(jnp.sqrt(inten[rows]), amp_floor)
            inten[rows] = live * (amps[u, rows].astype(F32) / size - 1.0)

        by_rows(factor_rows)

        if u == 1:
            g1w.wait_recv()

            def weight_rows(rows):
                plane_sum[last, rows] = (weight[rows] + core_in[last, rows].astype(F32)).astype(BF)

            by_rows(weight_rows)

            @pl.loop(1, XY)
            def _(step):
                g2w(step).start()

        @pl.loop(0, NT)
        def _(i):
            for turn in range(2):
                cc = core if turn else 1 - core
                m = 2 * i + cc

                def change_rows(rows):
                    factor = inten[rows]
                    wave[rows, 0:W] = (factor * far[m, rows, 0:W]).astype(BF)
                    wave[rows, W:] = (factor * far[m, rows, W:]).astype(BF)

                by_rows(change_rows)
                near[...] = transform(right_b, left_b)

                def near_rows(rows):
                    pr = modes[i, cc, 0, rows].astype(F32)
                    pi = modes[i, cc, 1, rows].astype(F32)
                    wr, wi = win[0, rows], win[1, rows]
                    nr, ni = near[rows, 0:W], near[rows, W:]
                    numer[u, 0, rows] += pr * nr + pi * ni
                    numer[u, 1, rows] += pr * ni - pi * nr
                    both = (wr * nr + wi * ni, wr * ni - wi * nr)
                    for p in range(2):
                        if u == 0:
                            grads[i, cc, p, rows] = both[p]
                        elif turn == 0:
                            core_out[2 * i + p, rows] = (grads[i, cc, p, rows] + both[p]).astype(BF)
                        else:
                            grads[i, cc, p, rows] += both[p]

                by_rows(near_rows)
                if u == 1 and turn == 0:
                    g1(i).start()

            if u == 1:
                g1(i).wait_recv()

                def sum_rows(rows):
                    for p in range(2):
                        k = 2 * i + p
                        plane_sum[k, rows] = (grads[i, core, p, rows] + core_in[k, rows].astype(F32)).astype(BF)

                by_rows(sum_rows)

                @pl.loop(1, XY)
                def _(step):
                    g2(i, step).start()

        for p in range(2):
            rolled = pltpu.roll(numer[u, p], lane, 1)
            rolled = pltpu.roll(rolled, row, 0)
            numer[u, p] = rolled
            pass_out[u, p] = rolled.astype(BF)

        @pl.when(has_next)
        def _():
            pass_sum(u).start()

    @pl.when(has_prev)
    def _():
        for item in prev_copies:
            item.wait()

    illum[...] = jnp.zeros((W, W), F32)
    for where_is, upper in ((place, True), (place_prev, False)):
        @pl.loop(0, 8)
        def _(slot):
            row, lane, block, live = where_is(slot)
            moved = pltpu.roll(pltpu.roll(power[...], lane, 1), row, 0)
            cols = jnp.where(col_id >= lane, block, block + 1) == t
            rows = (row_id >= row) if upper else (row_id < row)
            illum[...] += live * jnp.where(cols & rows, moved, 0.0)

    @pl.loop(1, XY)
    def _(step):
        source = lax.rem(q + step, XY)
        copy_to(plane_sum.at[last, shard], plane_in.at[source, last], gw_s.at[source], gw_r.at[source], s, right).wait_recv()

        @pl.loop(0, NT)
        def _(i):
            planes = pl.ds(2 * i, 2)
            copy_to(
                plane_sum.at[planes, shard], plane_in.at[source, planes],
                g2_s.at[i, source], g2_r.at[i, source], s, right,
            ).wait_recv()

    plane_in[q] = plane_sum[:, shard]
    for k in range(2 * NT + 1):
        value = plane_in[0, k].astype(F32)
        for source in range(1, XY):
            value = value + plane_in[source, k].astype(F32)
        if k < 2 * NT:
            z_out[k // 2, k % 2] = value.astype(BF)
        else:
            for i in range(NT):
                z_out[i, 2] = value.astype(BF)
    me_z = 2 * t + zlo
    z_in[me_z] = z_out[0]
    z_copies = []
    for flip in range(2):
        for d in range(NT):
            if flip == 0 and d == 0:
                continue
            k = flip * NT + d
            scan = other_zlo if flip else s
            item = copy_to(z_out.at[d], z_in.at[me_z], g3_s.at[k], g3_r.at[me_z], scan, lax.rem(t + d, NT))
            item.start()
            z_copies.append(item)

    @pl.when(has_prev)
    def _():
        for u in range(2):
            copy_to(pass_out.at[u], pass_in.at[u], np_s.at[u], np_r.at[u], s - 1, t).wait_recv()

    order = (opp, right, left, t)
    spots = [place(t + 4 * u) for u in range(2)] + [place_prev(t + 4 * u) for u in range(2)]

    def total_rows(rows):
        start = rows.start
        row_at = lax.broadcasted_iota(jnp.int32, (C, W), 0) + start
        col_at = lax.broadcasted_iota(jnp.int32, (C, W), 1)
        owners = [jnp.where(col_at >= lane, first, first + 1) for _, lane, first, _ in spots]
        for p in range(2):
            values = [numer[u, p, rows] for u in range(2)] + [pass_in[u, p, rows].astype(F32) for u in range(2)]
            values = [
                jnp.where(row_at >= spot[0] if k < 2 else row_at < spot[0], value, 0.0)
                for k, (value, spot) in enumerate(zip(values, spots))
            ]
            for slot, block in enumerate(order):
                value = 0.0
                for k in range(4):
                    value = value + jnp.where(owners[k] == block, values[k], 0.0)
                if slot == 0:
                    fwd_out[p, rows] = value.astype(BF)
                elif slot == 3:
                    total[2, p, rows] = value
                elif p == 2 - slot:
                    rs_out[slot - 1, p, rows] = value.astype(BF)
                else:
                    total[slot - 1, 0, rows] = value

    by_rows(total_rows)
    forwards = []
    for p, to in ((0, right), (1, left)):
        item = copy_to(fwd_out.at[p], fwd_in.at[p], nf_s.at[p], nf_r.at[p], s, to)
        item.start()
        forwards.append(item)
    sends = {}
    for way, to in ((0, right), (1, left)):
        for p in range(2):
            sends[way, p] = copy_to(
                rs_out.at[way, p], rs_in.at[way, p], nr_s.at[way, p], nr_r.at[way, p], s, to
            )
    sends[0, 1].start()
    sends[1, 0].start()
    for way in range(2):
        forwards[way].wait_recv()
        rs_out[way, way] = (total[way, 0] + fwd_in[way].astype(F32)).astype(BF)
        sends[way, way].start()

    for flip in range(2):
        for d in range(NT):
            if flip == 0 and d == 0:
                continue
            source = 2 * lax.rem(t + d, NT) + (1 - zlo if flip else zlo)
            copy_to(z_out.at[d], z_in.at[source], g3_s.at[d], g3_r.at[source], s, right).wait_recv()
    summed = [z_in[0, k].astype(F32) for k in range(3)]
    for source in range(1, 2 * NT):
        summed = [summed[k] + z_in[source, k].astype(F32) for k in range(3)]
    for p in range(2):
        step_full[core, p, shard] = summed[p] / (summed[2] + damping)

    def g4(step):
        to, device = column(step)
        src = step_full.at[core, :, shard]
        return copy_to(src, src, g4_s.at[to], g4_r.at[q], device, t)

    @pl.loop(1, XY)
    def _(step):
        g4(step).start()

    @pl.loop(1, XY)
    def _(step):
        source = lax.rem(q + step, XY)
        dst = step_full.at[core, :, shard_of(source)]
        copy_to(dst, dst, g4_s.at[source], g4_r.at[source], s, right).wait_recv()

    g5 = copy_to(step_full.at[core], step_full.at[core], g5_s, g5_r, other_core, t)
    g5.start()

    for item in sends.values():
        item.wait_recv()

    def object_rows(rows):
        scale = illum[rows] + damping
        for p in range(2):
            value = total[2, p, rows] + (rs_in[0, p, rows].astype(F32) + rs_in[1, p, rows].astype(F32))
            out_obj[p, rows] = obj[p, rows] + value / scale

    by_rows(object_rows)
    copy_to(step_full.at[1 - core], step_full.at[1 - core], g5_s, g5_r, other_core, t).wait_recv()
    out_probe[...] = step_full[...]

    for item in to_right + to_left + [on_right, on_left, g1w, g5] + forwards + z_copies + list(sends.values()):
        item.wait_send()
    for d in range(1, NT):
        copy_to(
            modes.at[0, core, :, shard], modes.at[NT - d, core, :, shard],
            pz_s.at[d], pz_r.at[NT - d], s, lax.rem(t + d, NT),
        ).wait_send()
        to_core(d).wait_send()

    @pl.loop(0, NT)
    def _(i):
        g1(i).wait_send()

    @pl.loop(1, XY)
    def _(step):
        over_columns(step).wait_send()
        g2w(step).wait_send()
        g4(step).wait_send()

        @pl.loop(0, NT)
        def _(i):
            g2(i, step).wait_send()

    @pl.when(has_prev)
    def _():
        for block in (t, left, right, opp):
            for p in range(2):
                passed(block, p).wait_send()

    @pl.when(has_next)
    def _():
        for item in tables:
            item.wait_send()
        for u in range(2):
            pass_sum(u).wait_send()


def shards(NS, NT, object_field, probe_modes, amplitudes, positions, counts):
    W = amplitudes.shape[1]
    XY = NS // 4
    R = W // XY
    fr, fi = dft_tables(W)
    vmem = pl.BlockSpec(memory_space=pltpu.VMEM)
    smem = pl.BlockSpec(memory_space=pltpu.SMEM)
    hbm = pl.BlockSpec(memory_space=pl.ANY)
    dma = pltpu.SemaphoreType.DMA

    def buf(*shape, dtype=F32):
        return pltpu.VMEM(shape, dtype)

    scratch = [
        buf(2, W, W), buf(2, 2, W, W),
        buf(NT, 2, W, W, dtype=BF), buf(NT, 2, W, W, dtype=BF), buf(NT, 2, 2, W, W, dtype=BF),
        buf(2, W, W, dtype=BF), buf(2 * W, 2 * W, dtype=BF), buf(2 * W, 2 * W, dtype=BF),
        buf(W, 2 * W, dtype=BF), buf(W, 2 * W, dtype=BF),
        buf(W, 2 * W, dtype=BF), buf(2 * W, 2 * W, dtype=BF), buf(2 * NT, W, 2 * W), buf(W, 2 * W),
        buf(W, W), buf(2, W, W), buf(2, 2, W, W), buf(NT, 2, 2, W, W), buf(W, W), buf(W, W), buf(W, W),
        buf(8, 2, dtype=jnp.int32), buf(1, dtype=jnp.int32),
        pltpu.SMEM((8, 2), jnp.int32), pltpu.SMEM((1,), jnp.int32),
        buf(2, 2, W, W, dtype=BF), buf(2, 2, W, W, dtype=BF), buf(3, 2, W, W),
        buf(2, W, W, dtype=BF), buf(2, W, W, dtype=BF), buf(2, 2, W, W, dtype=BF), buf(2, 2, W, W, dtype=BF),
        buf(2 * NT + 1, W, W, dtype=BF), buf(2 * NT + 1, W, W, dtype=BF), buf(2 * NT + 1, W, W, dtype=BF),
        buf(XY, 2 * NT + 1, R, W, dtype=BF), buf(NT, 3, R, W, dtype=BF), buf(2 * NT, 3, R, W, dtype=BF),
        buf(2, 2, W, W),
        dma((4,)), dma((2,)), dma((2,)), dma((2,)), dma((4,)), dma((4,)), dma((2,)), dma((2,)), dma((4, 2)), dma((4, 2)),
        dma((NT,)), dma((NT,)), dma((XY,)), dma((XY,)), dma((NT,)), dma((NT,)),
        dma((2,)), dma((2,)), dma((2,)), dma((2,)), dma((2, 2)), dma((2, 2)),
        dma((NT + 1,)), dma((NT + 1,)), dma((NT, XY)), dma((NT, XY)), dma((XY,)), dma((XY,)),
        dma((2 * NT,)), dma((2 * NT,)), dma((XY,)), dma((XY,)), dma, dma,
    ]
    new_object, probe_step = pl.pallas_call(
        functools.partial(kernel, W, XY, NS, NT),
        out_shape=(
            jax.ShapeDtypeStruct(object_field.shape, F32),
            jax.ShapeDtypeStruct(probe_modes.shape, F32),
        ),
        in_specs=[hbm, hbm, hbm, smem, smem, vmem, vmem, vmem, vmem],
        out_specs=(vmem, vmem),
        scratch_shapes=scratch,
        compiler_params=pltpu.CompilerParams(
            collective_id=0, has_side_effects=True, vmem_limit_bytes=58 * 1024 * 1024
        ),
    )(object_field, probe_modes, amplitudes, positions, counts, positions, counts, jnp.asarray(fr), jnp.asarray(fi))
    return new_object, probe_step


def solution(mesh):
    placed = (
        P(None, "scan", "tile"),
        P("tile", None, None, None),
        P("scan", None, None),
        P("scan", None),
        P("scan"),
    )
    return jax.shard_map(
        functools.partial(shards, mesh.shape["scan"], mesh.shape["tile"]),
        mesh=mesh,
        in_specs=placed,
        out_specs=(P(None, "scan", "tile"), P("tile", None, None, None)),
        check_vma=False,
    )
```

time: 142 us -> 115 us (0.81)
  the two profiles are of different devices: /device:TPU:1 before, /device:TPU:33 now
where the time goes in v2:
time: 115 us
  Pallas kernels  110 us (96%)
  local copies, waits for them, and re-layouts  3.62 us (3%)
  between operations  1.31 us (1%)
    pallas_call x1, Pallas kernels, shards(): pl.pallas_call(functools.partial(kernel, W, XY, NS, NT), out_shape=(jax.S...  110 us
    unnamed x7, local copies, waits for them, and re-layouts  3.62 us

profile of v2, /device:TPU:33, one launch (start us, length us, event | category | flops | bytes accessed | tf_op | source)
XLA Modules:
  0.0 115.1 jit_solution(15535850317660776804)
XLA Ops:
  0.6 0.0 copy-start.1
  1.3 0.0 copy-done.1
  1.3 0.7 copy.9.pos.pos_hbm
  2.0 110.2 %shard_map.86 = (f32[2,256,256]{2,1,0:T(8,128)}, f32[2,2,256,256]{3,2,1,0:T(8,128)}) custom-call(f32[2,256,256]{2,1,0:T(8,128)} %obj_hbm.1, f32[2,2,256,256]{3,2,1,0:T(8,128)} %probe_hbm.1, bf16[8,256,256]{2,1,0:T(8,128)(2,1)} %amp_hbm.1, s32[8,2]{1,0:T(8,128)} %copy.9.pos.pos_hbm, s32[1]{0:T(128)S(6)} %copy.13.cnt.cnt_hbm, s32[8,2]{1,0:T(8,128)} %copy.9.pos.pos_hbm, ...), custom_call_target="tpu_custom_call" | custom-call | tf_op jit(solution)/shard_map/pallas_call | solution.py:623
  112.2 0.0 copy-start
  112.2 2.0 %copy.14 = f32[2,256,256]{2,1,0:T(8,128)} copy(f32[2,256,256]{2,1,0:T(8,128)} %get-tuple-element.4) | data formatting | bytes 1048576
  114.1 0.0 copy-done
  114.1 1.0 copy.15
Async XLA Ops:
  0.6 0.7 copy-start.1
  112.2 2.0 %copy-start = (f32[2,2,256,256]{3,2,1,0:T(8,128)S(1)}, f32[2,2,256,256]{3,2,1,0:T(8,128)}, u32[]{:S(2)}) copy-start(f32[2,2,256,256]{3,2,1,0:T(8,128)} %get-tuple-element.5) | copy-start | bytes 3145732

commit v3 on v2

--- a/solution.py
+++ b/solution.py
@@ -27,15 +27,15 @@
     W, XY, NS, NT,
     obj_hbm, probe_hbm, amp_hbm, pos, cnt, pos_hbm, cnt_hbm, fr, fi,
     out_obj, out_probe,
-    obj, probe, band_a, band_b, modes, amps, right_f, right_b, left_f, left_b,
+    obj, probe, band_a, band_b, modes, amps, amps_t, right_f, right_b,
     wave, stack, far, near, inten, win, numer, grads, weight, power, illum,
     pos_land, cnt_land, prev_pos, prev_cnt,
     pass_out, pass_in, total, fwd_out, fwd_in, rs_out, rs_in,
-    core_out, core_in, plane_sum, plane_in, z_out, z_in, step_full,
+    core_out, core_in, plane_sum, plane_in, z_out, zw_out, z_in, zw_in, step_full,
     in_sem, sm_sem, tb_s, tb_r, ag_s, ag_r, fw_s, fw_r, ps_s, ps_r,
     pz_s, pz_r, px_s, px_r, pc_s, pc_r,
     np_s, np_r, nf_s, nf_r, nr_s, nr_r,
-    g1_s, g1_r, g2_s, g2_r, gw_s, gw_r, g3_s, g3_r, g4_s, g4_r, g5_s, g5_r,
+    g1_s, g1_r, g2_s, g2_r, gw_s, gw_r, g3_s, g3_r, zw_s, zw_r, g4_s, g4_r, g5_s, g5_r,
 ):
     R = W // XY
     C = min(32, W)
@@ -61,6 +61,10 @@
         to = lax.rem(q + step, XY)
         return to, to * 4 + zlo * 2 + core
 
+    def all_rows(body):
+        for step in range(W // C):
+            body(pl.ds(step * C, C))
+
     def by_rows(body):
         @pl.loop(0, W // C)
         def _(step):
@@ -186,10 +190,9 @@
         ref[0:W, W:] = fi[...] * sign
         ref[W:, 0:W] = fi[...] * -sign
         ref[W:, W:] = fr[...]
-    left_f[:, 0:W] = fr[...]
-    left_f[:, W:] = -fi[...]
-    left_b[:, 0:W] = fr[...]
-    left_b[:, W:] = fi[...]
+    for u in range(2):
+        local[2 + u].wait()
+        amps_t[u] = amps[u].astype(F32).T
 
     opp_first.wait_recv()
     start_pass(opp, 0)
@@ -220,9 +223,6 @@
             item.wait_recv()
             copy.start()
 
-    for item in local[2:]:
-        item.wait()
-
     @pl.when(has_next)
     def _():
         for block in (t, left, right, opp):
@@ -245,12 +245,14 @@
         live = jnp.where(has_prev & (slot < prev_cnt[0]), 1.0, 0.0).astype(F32)
         return row, lax.rem(col, W), col // W, live
 
-    def transform(right_table, left_table):
-        half = jnp.dot(wave[...], right_table[...], preferred_element_type=F32).astype(BF)
-        stack[0:W, :] = half
-        stack[W:, 0:W] = half[:, W:]
-        stack[W:, W:] = -half[:, 0:W]
-        return jnp.dot(left_table[...], stack[...], preferred_element_type=F32)
+    def transform(table, turned):
+        for k in range(2):
+            half = lax.dot_general(
+                turned[...], wave[k], (((1,), (1,)), ((), ())), preferred_element_type=F32
+            ).astype(BF)
+            stack[k * W : (k + 1) * W, 0:W] = half[0:W]
+            stack[k * W : (k + 1) * W, W:] = half[W:]
+        return jnp.dot(stack[...], table[...], preferred_element_type=F32)
 
     def pass_sum(u):
         return copy_to(pass_out.at[u], pass_in.at[u], np_s.at[u], np_r.at[u], s + 1, t)
@@ -276,6 +278,65 @@
     def g2w(step):
         to, device = column(step)
         return copy_to(plane_sum.at[last, shard_of(to)], plane_in.at[q, last], gw_s.at[to], gw_r.at[q], device, t)
+
+    me_z = 2 * t + zlo
+
+    def g3(i, flip):
+        return copy_to(
+            z_out.at[i], z_in.at[me_z], g3_s.at[i, flip], g3_r.at[me_z],
+            other_zlo if flip else s, lax.rem(t + i, NT),
+        )
+
+    def zw(k):
+        flip, d = k // NT, lax.rem(k, NT)
+        return copy_to(
+            zw_out, zw_in.at[me_z], zw_s.at[k], zw_r.at[me_z],
+            s + flip * (other_zlo - s), lax.rem(t + d, NT),
+        )
+
+    def reduce(i):
+        planes = pl.ds(2 * i, 2)
+
+        @pl.loop(1, XY)
+        def _(step):
+            source = lax.rem(q + step, XY)
+            copy_to(
+                plane_sum.at[planes, shard], plane_in.at[source, planes],
+                g2_s.at[i, source], g2_r.at[i, source], s, right,
+            ).wait_recv()
+
+        plane_in[q, planes] = plane_sum[planes, shard]
+        for p in range(2):
+            value = plane_in[0, 2 * i + p].astype(F32)
+            for source in range(1, XY):
+                value = value + plane_in[source, 2 * i + p].astype(F32)
+            z_out[i, p] = value.astype(BF)
+        g3(i, 1).start()
+
+        @pl.when(i > 0)
+        def _():
+            g3(i, 0).start()
+
+        @pl.when(i == 0)
+        def _():
+            z_in[me_z] = z_out[0]
+
+    def reduce_weight():
+        @pl.loop(1, XY)
+        def _(step):
+            source = lax.rem(q + step, XY)
+            copy_to(plane_sum.at[last, shard], plane_in.at[source, last], gw_s.at[source], gw_r.at[source], s, right).wait_recv()
+
+        plane_in[q, last] = plane_sum[last, shard]
+        value = plane_in[0, last].astype(F32)
+        for source in range(1, XY):
+            value = value + plane_in[source, last].astype(F32)
+        zw_out[...] = value.astype(BF)
+        zw_in[me_z] = zw_out[...]
+
+        @pl.loop(1, 2 * NT)
+        def _(k):
+            zw(k).start()
 
     for u in range(2):
         row, lane, block, live = place(t + 4 * u)
@@ -302,36 +363,41 @@
         if u == 1:
             g1w.start()
 
-        @pl.loop(0, 2 * NT)
-        def _(m):
-            i, cc = m // 2, lax.rem(m, 2)
+        @pl.loop(0, NT)
+        def _(i):
             if u == 0:
-                @pl.when((i > 0) & (cc == 0))
+                @pl.when(i > 0)
                 def _():
                     copy_to(modes.at[i, 1 - core], modes.at[i, 1 - core], pc_s.at[i], pc_r.at[i], other_core, t).wait_recv()
 
             def exit_rows(rows):
-                pr = modes[i, cc, 0, rows].astype(F32)
-                pi = modes[i, cc, 1, rows].astype(F32)
                 wr, wi = win[0, rows], win[1, rows]
-                wave[rows, 0:W] = (pr * wr - pi * wi).astype(BF)
-                wave[rows, W:] = (pr * wi + pi * wr).astype(BF)
+                square = 0.0
+                for cc in range(2):
+                    pr = modes[i, cc, 0, rows].astype(F32)
+                    pi = modes[i, cc, 1, rows].astype(F32)
+                    wave[cc, rows, 0:W] = (pr * wr - pi * wi).astype(BF)
+                    wave[cc, rows, W:] = (pr * wi + pi * wr).astype(BF)
+                    square = square + (pr * pr + pi * pi)
                 if u == 0:
-                    square = pr * pr + pi * pi
-                    power[rows] = jnp.where(m == 0, 0.0, power[rows]) + square
-
-            by_rows(exit_rows)
-            far[m] = transform(right_f, left_f)
+                    power[rows] = jnp.where(i == 0, 0.0, power[rows]) + square
+
+            all_rows(exit_rows)
+            far[i] = transform(right_f, right_b)
 
             def add_rows(rows):
-                fa, fb = far[m, rows, 0:W], far[m, rows, W:]
-                inten[rows] += fa * fa + fb * fb
-
-            by_rows(add_rows)
+                value = inten[rows]
+                for cc in range(2):
+                    both = pl.ds(rows.start + cc * W, C)
+                    fa, fb = far[i, both, 0:W], far[i, both, W:]
+                    value = value + (fa * fa + fb * fb)
+                inten[rows] = value
+
+            all_rows(add_rows)
 
         def factor_rows(rows):
             size = jnp.maximum(jnp.sqrt(inten[rows]), amp_floor)
-            inten[rows] = live * (amps[u, rows].astype(F32) / size - 1.0)
+            inten[rows] = live * (amps_t[u, rows] / size - 1.0)
 
         by_rows(factor_rows)
 
@@ -347,53 +413,68 @@
             def _(step):
                 g2w(step).start()
 
+        def finish(i):
+            g1(i).wait_recv()
+
+            def sum_rows(rows):
+                for p in range(2):
+                    k = 2 * i + p
+                    plane_sum[k, rows] = (grads[i, core, p, rows] + core_in[k, rows].astype(F32)).astype(BF)
+
+            by_rows(sum_rows)
+
+            @pl.loop(1, XY)
+            def _(step):
+                g2(i, step).start()
+
         @pl.loop(0, NT)
         def _(i):
-            for turn in range(2):
-                cc = core if turn else 1 - core
-                m = 2 * i + cc
-
-                def change_rows(rows):
-                    factor = inten[rows]
-                    wave[rows, 0:W] = (factor * far[m, rows, 0:W]).astype(BF)
-                    wave[rows, W:] = (factor * far[m, rows, W:]).astype(BF)
-
-                by_rows(change_rows)
-                near[...] = transform(right_b, left_b)
-
+            turns = (1 - core, core)
+
+            def change_rows(rows):
+                factor = inten[rows]
+                for turn, cc in enumerate(turns):
+                    both = pl.ds(rows.start + pl.multiple_of(cc * W, W), C)
+                    wave[turn, rows, 0:W] = (factor * far[i, both, 0:W]).astype(BF)
+                    wave[turn, rows, W:] = (factor * far[i, both, W:]).astype(BF)
+
+            all_rows(change_rows)
+            near[...] = transform(right_b, right_f)
+
+            for turn, cc in enumerate(turns):
                 def near_rows(rows):
+                    both = pl.ds(rows.start + turn * W, C)
                     pr = modes[i, cc, 0, rows].astype(F32)
                     pi = modes[i, cc, 1, rows].astype(F32)
                     wr, wi = win[0, rows], win[1, rows]
-                    nr, ni = near[rows, 0:W], near[rows, W:]
+                    nr, ni = near[both, 0:W], near[both, W:]
                     numer[u, 0, rows] += pr * nr + pi * ni
                     numer[u, 1, rows] += pr * ni - pi * nr
-                    both = (wr * nr + wi * ni, wr * ni - wi * nr)
+                    step = (wr * nr + wi * ni, wr * ni - wi * nr)
                     for p in range(2):
                         if u == 0:
-                            grads[i, cc, p, rows] = both[p]
+                            grads[i, cc, p, rows] = step[p]
                         elif turn == 0:
-                            core_out[2 * i + p, rows] = (grads[i, cc, p, rows] + both[p]).astype(BF)
+                            core_out[2 * i + p, rows] = (grads[i, cc, p, rows] + step[p]).astype(BF)
                         else:
-                            grads[i, cc, p, rows] += both[p]
-
-                by_rows(near_rows)
+                            grads[i, cc, p, rows] += step[p]
+
+                all_rows(near_rows)
                 if u == 1 and turn == 0:
                     g1(i).start()
 
+                    @pl.when(i > 0)
+                    def _():
+                        finish(i - 1)
+
             if u == 1:
-                g1(i).wait_recv()
-
-                def sum_rows(rows):
-                    for p in range(2):
-                        k = 2 * i + p
-                        plane_sum[k, rows] = (grads[i, core, p, rows] + core_in[k, rows].astype(F32)).astype(BF)
-
-                by_rows(sum_rows)
-
-                @pl.loop(1, XY)
-                def _(step):
-                    g2(i, step).start()
+                @pl.when(i == NT - 2)
+                def _():
+                    reduce_weight()
+
+                @pl.when(i > 1)
+                def _():
+                    reduce(i - 2)
 
         for p in range(2):
             rolled = pltpu.roll(numer[u, p], lane, 1)
@@ -405,13 +486,15 @@
         def _():
             pass_sum(u).start()
 
+    finish(NT - 1)
+    reduce(NT - 2)
+
     @pl.when(has_prev)
     def _():
         for item in prev_copies:
             item.wait()
 
-    illum[...] = jnp.zeros((W, W), F32)
-    for where_is, upper in ((place, True), (place_prev, False)):
+    def illuminate(where_is, upper):
         @pl.loop(0, 8)
         def _(slot):
             row, lane, block, live = where_is(slot)
@@ -420,41 +503,8 @@
             rows = (row_id >= row) if upper else (row_id < row)
             illum[...] += live * jnp.where(cols & rows, moved, 0.0)
 
-    @pl.loop(1, XY)
-    def _(step):
-        source = lax.rem(q + step, XY)
-        copy_to(plane_sum.at[last, shard], plane_in.at[source, last], gw_s.at[source], gw_r.at[source], s, right).wait_recv()
-
-        @pl.loop(0, NT)
-        def _(i):
-            planes = pl.ds(2 * i, 2)
-            copy_to(
-                plane_sum.at[planes, shard], plane_in.at[source, planes],
-                g2_s.at[i, source], g2_r.at[i, source], s, right,
-            ).wait_recv()
-
-    plane_in[q] = plane_sum[:, shard]
-    for k in range(2 * NT + 1):
-        value = plane_in[0, k].astype(F32)
-        for source in range(1, XY):
-            value = value + plane_in[source, k].astype(F32)
-        if k < 2 * NT:
-            z_out[k // 2, k % 2] = value.astype(BF)
-        else:
-            for i in range(NT):
-                z_out[i, 2] = value.astype(BF)
-    me_z = 2 * t + zlo
-    z_in[me_z] = z_out[0]
-    z_copies = []
-    for flip in range(2):
-        for d in range(NT):
-            if flip == 0 and d == 0:
-                continue
-            k = flip * NT + d
-            scan = other_zlo if flip else s
-            item = copy_to(z_out.at[d], z_in.at[me_z], g3_s.at[k], g3_r.at[me_z], scan, lax.rem(t + d, NT))
-            item.start()
-            z_copies.append(item)
+    illum[...] = jnp.zeros((W, W), F32)
+    illuminate(place, True)
 
     @pl.when(has_prev)
     def _():
@@ -502,6 +552,8 @@
             )
     sends[0, 1].start()
     sends[1, 0].start()
+    reduce(NT - 1)
+    illuminate(place_prev, False)
     for way in range(2):
         forwards[way].wait_recv()
         rs_out[way, way] = (total[way, 0] + fwd_in[way].astype(F32)).astype(BF)
@@ -512,10 +564,12 @@
             if flip == 0 and d == 0:
                 continue
             source = 2 * lax.rem(t + d, NT) + (1 - zlo if flip else zlo)
-            copy_to(z_out.at[d], z_in.at[source], g3_s.at[d], g3_r.at[source], s, right).wait_recv()
-    summed = [z_in[0, k].astype(F32) for k in range(3)]
-    for source in range(1, 2 * NT):
-        summed = [summed[k] + z_in[source, k].astype(F32) for k in range(3)]
+            copy_to(z_out.at[d], z_in.at[source], g3_s.at[d, 0], g3_r.at[source], s, right).wait_recv()
+            copy_to(zw_out, zw_in.at[source], zw_s.at[d], zw_r.at[source], s, right).wait_recv()
+    parts = [[z_in[k, 0], z_in[k, 1], zw_in[k]] for k in range(2 * NT)]
+    summed = [item.astype(F32) for item in parts[0]]
+    for part in parts[1:]:
+        summed = [value + item.astype(F32) for value, item in zip(summed, part)]
     for p in range(2):
         step_full[core, p, shard] = summed[p] / (summed[2] + damping)
 
@@ -550,7 +604,7 @@
     copy_to(step_full.at[1 - core], step_full.at[1 - core], g5_s, g5_r, other_core, t).wait_recv()
     out_probe[...] = step_full[...]
 
-    for item in to_right + to_left + [on_right, on_left, g1w, g5] + forwards + z_copies + list(sends.values()):
+    for item in to_right + to_left + [on_right, on_left, g1w, g5] + forwards + list(sends.values()):
         item.wait_send()
     for d in range(1, NT):
         copy_to(
@@ -558,6 +612,15 @@
             pz_s.at[d], pz_r.at[NT - d], s, lax.rem(t + d, NT),
         ).wait_send()
         to_core(d).wait_send()
+
+    for i in range(NT):
+        g3(i, 1).wait_send()
+        if i > 0:
+            g3(i, 0).wait_send()
+
+    @pl.loop(1, 2 * NT)
+    def _(k):
+        zw(k).wait_send()
 
     @pl.loop(0, NT)
     def _(i):
@@ -603,22 +666,21 @@
     scratch = [
         buf(2, W, W), buf(2, 2, W, W),
         buf(NT, 2, W, W, dtype=BF), buf(NT, 2, W, W, dtype=BF), buf(NT, 2, 2, W, W, dtype=BF),
-        buf(2, W, W, dtype=BF), buf(2 * W, 2 * W, dtype=BF), buf(2 * W, 2 * W, dtype=BF),
-        buf(W, 2 * W, dtype=BF), buf(W, 2 * W, dtype=BF),
-        buf(W, 2 * W, dtype=BF), buf(2 * W, 2 * W, dtype=BF), buf(2 * NT, W, 2 * W), buf(W, 2 * W),
+        buf(2, W, W, dtype=BF), buf(2, W, W), buf(2 * W, 2 * W, dtype=BF), buf(2 * W, 2 * W, dtype=BF),
+        buf(2, W, 2 * W, dtype=BF), buf(2 * W, 2 * W, dtype=BF), buf(NT, 2 * W, 2 * W), buf(2 * W, 2 * W),
         buf(W, W), buf(2, W, W), buf(2, 2, W, W), buf(NT, 2, 2, W, W), buf(W, W), buf(W, W), buf(W, W),
         buf(8, 2, dtype=jnp.int32), buf(1, dtype=jnp.int32),
         pltpu.SMEM((8, 2), jnp.int32), pltpu.SMEM((1,), jnp.int32),
         buf(2, 2, W, W, dtype=BF), buf(2, 2, W, W, dtype=BF), buf(3, 2, W, W),
         buf(2, W, W, dtype=BF), buf(2, W, W, dtype=BF), buf(2, 2, W, W, dtype=BF), buf(2, 2, W, W, dtype=BF),
         buf(2 * NT + 1, W, W, dtype=BF), buf(2 * NT + 1, W, W, dtype=BF), buf(2 * NT + 1, W, W, dtype=BF),
-        buf(XY, 2 * NT + 1, R, W, dtype=BF), buf(NT, 3, R, W, dtype=BF), buf(2 * NT, 3, R, W, dtype=BF),
+        buf(XY, 2 * NT + 1, R, W, dtype=BF), buf(NT, 2, R, W, dtype=BF), buf(R, W, dtype=BF), buf(2 * NT, 2, R, W, dtype=BF), buf(2 * NT, R, W, dtype=BF),
         buf(2, 2, W, W),
         dma((4,)), dma((2,)), dma((2,)), dma((2,)), dma((4,)), dma((4,)), dma((2,)), dma((2,)), dma((4, 2)), dma((4, 2)),
         dma((NT,)), dma((NT,)), dma((XY,)), dma((XY,)), dma((NT,)), dma((NT,)),
         dma((2,)), dma((2,)), dma((2,)), dma((2,)), dma((2, 2)), dma((2, 2)),
         dma((NT + 1,)), dma((NT + 1,)), dma((NT, XY)), dma((NT, XY)), dma((XY,)), dma((XY,)),
-        dma((2 * NT,)), dma((2 * NT,)), dma((XY,)), dma((XY,)), dma, dma,
+        dma((NT, 2)), dma((2 * NT,)), dma((2 * NT,)), dma((2 * NT,)), dma((XY,)), dma((XY,)), dma, dma,
     ]
     new_object, probe_step = pl.pallas_call(
         functools.partial(kernel, W, XY, NS, NT),

time: 115 us -> 108 us (0.939)
  the two profiles are of different devices: /device:TPU:33 before, /device:TPU:1 now
where the time goes in v3:
time: 108 us
  Pallas kernels  103 us (95%)
  local copies, waits for them, and re-layouts  3.62 us (3%)
  between operations  1.31 us (1%)
    pallas_call x1, Pallas kernels, shards(): pl.pallas_call(functools.partial(kernel, W, XY, NS, NT), out_shape=(jax.S...  103 us
    unnamed x7, local copies, waits for them, and re-layouts  3.62 us

profile of v3, /device:TPU:1, one launch (start us, length us, event | category | flops | bytes accessed | tf_op | source)
XLA Modules:
  0.0 108.2 jit_solution(8767211145169218352)
XLA Ops:
  0.6 0.0 copy-start.1
  1.3 0.0 copy-done.1
  1.3 0.7 copy.9.pos.pos_hbm
  2.0 103.3 %shard_map.86 = (f32[2,256,256]{2,1,0:T(8,128)}, f32[2,2,256,256]{3,2,1,0:T(8,128)}) custom-call(f32[2,256,256]{2,1,0:T(8,128)} %obj_hbm.1, f32[2,2,256,256]{3,2,1,0:T(8,128)} %probe_hbm.1, bf16[8,256,256]{2,1,0:T(8,128)(2,1)} %amp_hbm.1, s32[8,2]{1,0:T(8,128)} %copy.9.pos.pos_hbm, s32[1]{0:T(128)S(6)} %copy.13.cnt.cnt_hbm, s32[8,2]{1,0:T(8,128)} %copy.9.pos.pos_hbm, ...), custom_call_target="tpu_custom_call" | custom-call | tf_op jit(solution)/shard_map/pallas_call | solution.py:685
  105.2 0.0 copy-start
  105.3 2.0 %copy.14 = f32[2,256,256]{2,1,0:T(8,128)} copy(f32[2,256,256]{2,1,0:T(8,128)} %get-tuple-element.4) | data formatting | bytes 1048576
  107.2 0.0 copy-done
  107.2 1.0 copy.15
Async XLA Ops:
  0.6 0.7 copy-start.1
  105.2 2.0 %copy-start = (f32[2,2,256,256]{3,2,1,0:T(8,128)S(1)}, f32[2,2,256,256]{3,2,1,0:T(8,128)}, u32[]{:S(2)}) copy-start(f32[2,2,256,256]{3,2,1,0:T(8,128)} %get-tuple-element.5) | copy-start | bytes 3145732

commit v4 on v3

--- a/solution.py
+++ b/solution.py
@@ -467,14 +467,6 @@
                     def _():
                         finish(i - 1)
 
-            if u == 1:
-                @pl.when(i == NT - 2)
-                def _():
-                    reduce_weight()
-
-                @pl.when(i > 1)
-                def _():
-                    reduce(i - 2)
 
         for p in range(2):
             rolled = pltpu.roll(numer[u, p], lane, 1)
@@ -487,7 +479,6 @@
             pass_sum(u).start()
 
     finish(NT - 1)
-    reduce(NT - 2)
 
     @pl.when(has_prev)
     def _():
@@ -504,7 +495,6 @@
             illum[...] += live * jnp.where(cols & rows, moved, 0.0)
 
     illum[...] = jnp.zeros((W, W), F32)
-    illuminate(place, True)
 
     @pl.when(has_prev)
     def _():
@@ -552,7 +542,10 @@
             )
     sends[0, 1].start()
     sends[1, 0].start()
-    reduce(NT - 1)
+    reduce_weight()
+    for i in range(NT):
+        reduce(i)
+    illuminate(place, True)
     illuminate(place_prev, False)
     for way in range(2):
         forwards[way].wait_recv()

time: 108 us -> 102 us (0.944)
  Pallas kernels: 103 us -> 96.9 us
    pallas_call x1, Pallas kernels: 103 us -> 96.9 us  [shards(): pl.pallas_call(functools.partial(kernel, W, XY, NS, NT), out_shape=(jax.S...]
where the time goes in v4:
time: 102 us
  Pallas kernels  96.9 us (95%)
  local copies, waits for them, and re-layouts  3.62 us (4%)
  between operations  1.31 us (1%)
    pallas_call x1, Pallas kernels, shards(): pl.pallas_call(functools.partial(kernel, W, XY, NS, NT), out_shape=(jax.S...  96.9 us
    unnamed x7, local copies, waits for them, and re-layouts  3.62 us

profile of v4, /device:TPU:1, one launch (start us, length us, event | category | flops | bytes accessed | tf_op | source)
XLA Modules:
  0.0 101.9 jit_solution(2601873784958965174)
XLA Ops:
  0.6 0.0 copy-start.1
  1.3 0.0 copy-done.1
  1.3 0.7 copy.9.pos.pos_hbm
  2.0 96.9 %shard_map.86 = (f32[2,256,256]{2,1,0:T(8,128)}, f32[2,2,256,256]{3,2,1,0:T(8,128)}) custom-call(f32[2,256,256]{2,1,0:T(8,128)} %obj_hbm.1, f32[2,2,256,256]{3,2,1,0:T(8,128)} %probe_hbm.1, bf16[8,256,256]{2,1,0:T(8,128)(2,1)} %amp_hbm.1, s32[8,2]{1,0:T(8,128)} %copy.9.pos.pos_hbm, s32[1]{0:T(128)S(6)} %copy.13.cnt.cnt_hbm, s32[8,2]{1,0:T(8,128)} %copy.9.pos.pos_hbm, ...), custom_call_target="tpu_custom_call" | custom-call | tf_op jit(solution)/shard_map/pallas_call | solution.py:678
  98.9 0.0 copy-start
  98.9 2.0 %copy.14 = f32[2,256,256]{2,1,0:T(8,128)} copy(f32[2,256,256]{2,1,0:T(8,128)} %get-tuple-element.4) | data formatting | bytes 1048576
  100.9 0.0 copy-done
  100.9 1.0 copy.15
Async XLA Ops:
  0.6 0.7 copy-start.1
  98.9 2.0 %copy-start = (f32[2,2,256,256]{3,2,1,0:T(8,128)S(1)}, f32[2,2,256,256]{3,2,1,0:T(8,128)}, u32[]{:S(2)}) copy-start(f32[2,2,256,256]{3,2,1,0:T(8,128)} %get-tuple-element.5) | copy-start | bytes 3145732
